TPU v7x, 32 devices: a whole 2x2x4 slice. The times are simulated.
32 devices in a mesh: dp: 8 (over z, x), tensor: 4 (over y, core).
Axes of the slice: x: 2, y: 2, z: 4, core: 2. Of those that a mesh axis runs over, the one named last changes fastest.
Arguments:
- tokens: bfloat16 [1024, 16, 1024], P(None, 'dp'), may hold values from -6 to 6
- condition: bfloat16 [16, 1024], P('dp'), may hold values from -6 to 6
- modulation_weight: bfloat16 [1024, 6144], replicated, may hold values from -0.1875 to 0.1875
- modulation_bias: bfloat16 [6144], replicated, may hold values from -3 to 3
- qkv_weight: bfloat16 [1024, 3, 1024], P(None, None, 'tensor'), may hold values from -0.1875 to 0.1875
- qv_bias: bfloat16 [2, 1024], P(None, 'tensor'), may hold values from -2 to 2
- proj_weight: bfloat16 [1024, 1024], P('tensor'), may hold values from -3 to 3
- proj_bias: bfloat16 [1024], replicated, may hold values from -6 to 6
- up_weight: bfloat16 [1024, 4096], P(None, 'tensor'), may hold values from -0.1875 to 0.1875
- up_bias: bfloat16 [4096], P('tensor'), may hold values from -3 to 3
- down_weight: bfloat16 [4096, 1024], P('tensor'), may hold values from -0.09375 to 0.09375
- down_bias: bfloat16 [1024], replicated, may hold values from -3 to 3
- cotangent: bfloat16 [1024, 16, 1024], P(None, 'dp'), may hold values from -6 to 6
Outputs:
- output: bfloat16 [1024, 16, 1024], P('tensor', 'dp')
- grad_tokens: float32 [1024, 16, 1024], P('tensor', 'dp')
- grad_condition: float32 [16, 1024], P('dp')
- grad_modulation_weight: float32 [1024, 6144], P('dp', 'tensor')
- grad_modulation_bias: float32 [6144], P('tensor')
- grad_qkv_weight: float32 [1024, 3, 1024], P('dp', None, 'tensor')
- grad_qv_bias: float32 [2, 1024], P(None, 'tensor')
- grad_proj_weight: float32 [1024, 1024], P('tensor', 'dp')
- grad_proj_bias: float32 [1024], replicated
- grad_up_weight: float32 [1024, 4096], P('dp', 'tensor')
- grad_up_bias: float32 [4096], P('tensor')
- grad_down_weight: float32 [4096, 1024], P('tensor', 'dp')
- grad_down_bias: float32 [1024], replicated
All inputs are finite; a program needn't handle non-finite values.
Results may differ from a plain program's by a relative error of at most 0.013.
The roundings to bfloat16 on the way count: a program that leaves them out, or rounds other values in their place, can miss the bound.
Values may be sent and summed in bfloat16 or wider, within the bound.
No kernel may reach another device: no remote copies, remote signals or barrier semaphores. Data moves between devices by JAX's collectives and lax.ppermute only.
A program may use at most 192 MiB of HBM per device.

v0:
```python
import jax
import jax.numpy as jnp
from jax import lax
from jax.sharding import PartitionSpec as P

HEAD_DIM = 64


EPS = 1e-06


def contract_rows(left, right):
    return lax.dot_general(
        left, right, (((0,), (0,)), ((), ())), preferred_element_type=jnp.float32
    )


def contract_cols(left, right):
    return lax.dot_general(
        left, right, (((1,), (1,)), ((), ())), preferred_element_type=jnp.float32
    )


def layer_norm(values):
    centre = values - jnp.mean(values, axis=-1, keepdims=True)
    inverse = lax.rsqrt(jnp.mean(centre * centre, axis=-1, keepdims=True) + EPS)
    return (centre * inverse, inverse)


def norm_back(grad_normed, normed, inverse):
    return inverse * (
        grad_normed
        - jnp.mean(grad_normed, axis=-1, keepdims=True)
        - normed * jnp.mean(grad_normed * normed, axis=-1, keepdims=True)
    )


def gelu_tanh(values):
    return jax.nn.gelu(values, approximate=True)


def attend_forward(query, key, value, block):
    scale = HEAD_DIM ** (-0.5)
    blocks = query.reshape((query.shape[0] // block, block) + query.shape[1:])

    def one_block(query_block):
        scores = (
            jnp.einsum("qlhd,klhd->lhqk", query_block, key, preferred_element_type=jnp.float32)
            * scale
        )
        largest = jnp.max(scores, axis=-1, keepdims=True)
        powers = jnp.exp(scores - largest)
        total = jnp.sum(powers, axis=-1, keepdims=True)
        probs = powers / total
        mixed = jnp.einsum(
            "lhqk,klhd->qlhd", probs.astype(jnp.bfloat16), value, preferred_element_type=jnp.float32
        )
        return (mixed.astype(jnp.bfloat16), (largest + jnp.log(total))[..., 0])

    mixed, log_total = lax.map(one_block, blocks)
    return (mixed.reshape(query.shape), log_total)


def attend_backward(query, key, value, log_total, grad_mixed, block):
    scale = HEAD_DIM ** (-0.5)
    shape = (query.shape[0] // block, block) + query.shape[1:]

    def one_block(carry, items):
        key_grad, value_grad = carry
        query_block, grad_block, total_block = items
        scores = (
            jnp.einsum("qlhd,klhd->lhqk", query_block, key, preferred_element_type=jnp.float32)
            * scale
        )
        probs = jnp.exp(scores - total_block[..., None])
        rounded = probs.astype(jnp.bfloat16)
        grad_probs = jnp.einsum(
            "qlhd,klhd->lhqk", grad_block, value, preferred_element_type=jnp.float32
        )
        inner = jnp.sum(probs * grad_probs, axis=-1, keepdims=True)
        grad_scores = (probs * (grad_probs - inner)).astype(jnp.bfloat16)
        query_grad = (
            jnp.einsum("lhqk,klhd->qlhd", grad_scores, key, preferred_element_type=jnp.float32)
            * scale
        ).astype(jnp.bfloat16)
        key_grad = (
            key_grad
            + jnp.einsum(
                "lhqk,qlhd->klhd", grad_scores, query_block, preferred_element_type=jnp.float32
            )
            * scale
        )
        value_grad = value_grad + jnp.einsum(
            "lhqk,qlhd->klhd", rounded, grad_block, preferred_element_type=jnp.float32
        )
        return ((key_grad, value_grad), query_grad)

    empty = jnp.zeros(key.shape, jnp.float32)
    (key_grad, value_grad), query_grad = lax.scan(
        one_block, (empty, empty), (query.reshape(shape), grad_mixed.reshape(shape), log_total)
    )
    return (
        query_grad.reshape(query.shape),
        key_grad.astype(jnp.bfloat16),
        value_grad.astype(jnp.bfloat16),
    )


def token_sum(values):
    return jnp.sum(values, axis=0)


def shards(
    tokens,
    condition,
    modulation_weight,
    modulation_bias,
    qkv_weight,
    qv_bias,
    proj_weight,
    proj_bias,
    up_weight,
    up_bias,
    down_weight,
    down_bias,
    cotangent,
):
    seq_len, lat_count, width = tokens.shape
    parts = lax.axis_size("tensor")
    place = lax.axis_index("tensor")
    quarter = seq_len // parts
    rows = seq_len * lat_count
    block = min(seq_len, 512)
    heads_here = qkv_weight.shape[2] // HEAD_DIM
    mod_cols = modulation_weight.shape[1] // parts
    cond_float = condition.astype(jnp.float32)
    silu_low = jax.nn.silu(cond_float).astype(jnp.bfloat16)
    modulation = (
        jnp.dot(silu_low, modulation_weight, preferred_element_type=jnp.float32)
        + modulation_bias.astype(jnp.float32)
    ).reshape(lat_count, 6, width)
    shift_one = modulation[:, 0]
    scale_one = modulation[:, 1]
    gate_one = modulation[:, 2]
    shift_two = modulation[:, 3]
    scale_two = modulation[:, 4]
    gate_two = modulation[:, 5]
    stream_in = tokens.astype(jnp.float32)
    normed_one, inverse_one = layer_norm(stream_in)
    attend_in = (normed_one * (1.0 + scale_one) + shift_one).astype(jnp.bfloat16)
    flat_in = attend_in.reshape(rows, width)
    qkv_flat = qkv_weight.reshape(width, -1)
    projected = jnp.dot(flat_in, qkv_flat, preferred_element_type=jnp.float32).reshape(
        seq_len, lat_count, 3, -1
    )
    bias_float = qv_bias.astype(jnp.float32)
    head_shape = (seq_len, lat_count, heads_here, HEAD_DIM)
    query = (projected[:, :, 0] + bias_float[0]).astype(jnp.bfloat16).reshape(head_shape)
    key = projected[:, :, 1].astype(jnp.bfloat16).reshape(head_shape)
    value = (projected[:, :, 2] + bias_float[1]).astype(jnp.bfloat16).reshape(head_shape)
    mixed, log_total = attend_forward(query, key, value, block)
    mixed_flat = mixed.reshape(rows, -1)
    attend_update = (
        lax.psum_scatter(
            jnp.dot(mixed_flat, proj_weight, preferred_element_type=jnp.float32),
            "tensor",
            scatter_dimension=0,
            tiled=True,
        )
        + proj_bias.astype(jnp.float32)
    ).reshape(quarter, lat_count, width)
    stream_here = lax.dynamic_slice_in_dim(stream_in, place * quarter, quarter, 0)
    stream = stream_here + gate_one * attend_update
    normed_two, inverse_two = layer_norm(stream)
    mlp_here = (normed_two * (1.0 + scale_two) + shift_two).astype(jnp.bfloat16)
    mlp_in = lax.all_gather(mlp_here, "tensor", axis=0, tiled=True).reshape(rows, width)
    hidden_pre = jnp.dot(mlp_in, up_weight, preferred_element_type=jnp.float32) + up_bias.astype(
        jnp.float32
    )
    hidden, gelu_pull = jax.vjp(gelu_tanh, hidden_pre)
    hidden_low = hidden.astype(jnp.bfloat16)
    mlp_update = (
        lax.psum_scatter(
            jnp.dot(hidden_low, down_weight, preferred_element_type=jnp.float32),
            "tensor",
            scatter_dimension=0,
            tiled=True,
        )
        + down_bias.astype(jnp.float32)
    ).reshape(quarter, lat_count, width)
    output = (stream + gate_two * mlp_update).astype(jnp.bfloat16)
    grad_here = lax.dynamic_slice_in_dim(cotangent, place * quarter, quarter, 0).astype(jnp.float32)
    grad_mlp = (gate_two * cotangent).astype(jnp.bfloat16).reshape(rows, width)
    grad_down_bias = jnp.sum(grad_mlp, axis=0, dtype=jnp.float32)
    grad_down_t = contract_rows(grad_mlp, hidden_low)
    grad_hidden = contract_cols(grad_mlp, down_weight)
    grad_pre = gelu_pull(grad_hidden)[0].astype(jnp.bfloat16)
    grad_up_bias = jnp.sum(grad_pre, axis=0, dtype=jnp.float32)
    grad_up = contract_rows(mlp_in, grad_pre)
    grad_mlp_in = lax.psum_scatter(
        contract_cols(grad_pre, up_weight), "tensor", scatter_dimension=0, tiled=True
    ).reshape(quarter, lat_count, width)
    up_shard, down_shard = (
        lax.psum_scatter(grad_up, "dp", scatter_dimension=0, tiled=True),
        lax.psum_scatter(grad_down_t, "dp", scatter_dimension=0, tiled=True),
    )
    up_bias_sum, down_bias_sum = lax.psum((grad_up_bias, grad_down_bias), "dp")
    grad_stream = grad_here + norm_back(grad_mlp_in * (1.0 + scale_two), normed_two, inverse_two)
    update_here = (gate_one * grad_stream).astype(jnp.bfloat16)
    grad_update = lax.all_gather(update_here, "tensor", axis=0, tiled=True).reshape(rows, width)
    grad_proj_bias = jnp.sum(grad_update, axis=0, dtype=jnp.float32)
    grad_proj_t = contract_rows(grad_update, mixed_flat)
    grad_mixed = contract_cols(grad_update, proj_weight).astype(jnp.bfloat16).reshape(head_shape)
    grad_query, grad_key, grad_value = attend_backward(
        query, key, value, log_total, grad_mixed, block
    )
    grad_qv_bias = jnp.stack(
        [
            jnp.sum(grad_query, axis=(0, 1), dtype=jnp.float32).reshape(-1),
            jnp.sum(grad_value, axis=(0, 1), dtype=jnp.float32).reshape(-1),
        ]
    )
    grad_qkv_flat = jnp.stack(
        [grad_query.reshape(rows, -1), grad_key.reshape(rows, -1), grad_value.reshape(rows, -1)],
        axis=1,
    ).reshape(rows, -1)
    grad_qkv = contract_rows(flat_in, grad_qkv_flat).reshape(width, 3, -1)
    grad_attend_in = lax.psum_scatter(
        contract_cols(grad_qkv_flat, qkv_flat), "tensor", scatter_dimension=0, tiled=True
    ).reshape(quarter, lat_count, width)
    normed_here = lax.dynamic_slice_in_dim(normed_one, place * quarter, quarter, 0)
    inverse_here = lax.dynamic_slice_in_dim(inverse_one, place * quarter, quarter, 0)
    grad_tokens = grad_stream + norm_back(
        grad_attend_in * (1.0 + scale_one), normed_here, inverse_here
    )
    mod_part = jnp.stack(
        [
            token_sum(grad_attend_in),
            token_sum(grad_attend_in * normed_here),
            token_sum(grad_stream * attend_update),
            token_sum(grad_mlp_in),
            token_sum(grad_mlp_in * normed_two),
            token_sum(grad_here * mlp_update),
        ],
        axis=1,
    ).reshape(lat_count, -1)
    grad_modulation = lax.psum(mod_part, "tensor").astype(jnp.bfloat16)
    grad_silu = contract_cols(grad_modulation, modulation_weight)
    grad_condition = jax.vjp(jax.nn.silu, cond_float)[1](grad_silu)[0]
    own_cols = lax.dynamic_slice_in_dim(grad_modulation, place * mod_cols, mod_cols, 1)
    grad_mod_weight = contract_rows(silu_low, own_cols)
    grad_mod_bias = jnp.sum(own_cols, axis=0, dtype=jnp.float32)
    mod_shard, qkv_shard, proj_shard = (
        lax.psum_scatter(grad_mod_weight, "dp", scatter_dimension=0, tiled=True),
        lax.psum_scatter(grad_qkv, "dp", scatter_dimension=0, tiled=True),
        lax.psum_scatter(grad_proj_t, "dp", scatter_dimension=0, tiled=True),
    )
    mod_bias_sum, qv_bias_sum, proj_bias_sum = lax.psum(
        (grad_mod_bias, grad_qv_bias, grad_proj_bias), "dp"
    )
    return (
        output,
        grad_tokens,
        grad_condition,
        mod_shard,
        mod_bias_sum,
        qkv_shard,
        qv_bias_sum,
        proj_shard.T,
        proj_bias_sum,
        up_shard,
        up_bias_sum,
        down_shard.T,
        down_bias_sum,
    )


def solution(mesh):
    in_specs = (
        P(None, "dp", None),
        P("dp", None),
        P(),
        P(),
        P(None, None, "tensor"),
        P(None, "tensor"),
        P("tensor", None),
        P(),
        P(None, "tensor"),
        P("tensor"),
        P("tensor", None),
        P(),
        P(None, "dp", None),
    )
    out_specs = (
        P("tensor", "dp", None),
        P("tensor", "dp", None),
        P("dp", None),
        P("dp", "tensor"),
        P("tensor"),
        P("dp", None, "tensor"),
        P(None, "tensor"),
        P("tensor", "dp"),
        P(),
        P("dp", "tensor"),
        P("tensor"),
        P("tensor", "dp"),
        P(),
    )
    return jax.shard_map(shards, mesh=mesh, in_specs=in_specs, out_specs=out_specs, check_vma=False)
```

profile of v0, /device:TPU:0, one launch (start us, length us, event | category | flops | bytes accessed | tf_op | source)
XLA Modules:
  0.0 1117.1 jit_solution(16225464052737840834)
XLA Ops:
  8.1 6.3 convolution_add_fusion
  15.1 5.9 convert_reduce_fusion.3
  21.1 7.5 multiply_reduce_fusion.2
  31.5 9.9 subtract_multiply_fusion
  47.6 4.0 squeeze.22
  56.9 24.7 %while.27 = (s32[]{:T(128)}, bf16[2,512,2,4,64]{1,4,3,2,0:T(8,128)(2,1)}, f32[2,2,4,512]{3,2,1,0:T(4,128)S(1)}, bf16[2,512,2,4,64]{1,4,3,2,0:T(8,128)(2,1)}, bf1...) while((s32[]{:T(128)}, bf16[2,512,2,4,64]{1,4,3,2,0:T(8,128)(2,1)}, ...), condition=%wide.region_5.6_spmd, body=%wide.region_2.5_spmd.sunk | while | flops 1111748608 | bytes 66191540 | solution.py:60
  63.9 4.4 fusion.122
  69.3 3.5 multiply_reduce_fusion.13
  76.3 4.4 fusion.122
  81.6 4.3 copy.74
  86.0 4.3 reshape_reshape.8
  90.3 5.8 fusion.67
  96.3 8.5 convert_element_type.118
  104.9 65.9 %reduce-scatter.10.cloned.1.call-done = f32[512,1024]{1,0:T(8,128)} async-done(((f32[2048,1024]{1,0:T(8,128)}), f32[512,1024]{1,0:T(8,128)}) %reduce-scatter.10.cloned.1.call-update) | async-done | bytes 2097168 | tf_op jit(solution)/shard_map/reduce_scatter | solution.py:164
  177.4 3.7 fusion.64
  185.8 10.8 convert_reduce_fusion
  196.5 7.4 reshape.203
  203.9 15.9 %all-gather.3.cloned.1.call-done = bf16[1024,2,1024]{2,1,0:T(2,128)(2,1)} async-done(((bf16[256,2,1024]{2,1,0:T(2,128)(2,1)}), bf16[1024,2,1024]{2,1,0:T(2,128)(2,1)}) %all-gather.3.cloned.1.call-update) | async-done | bytes 4194320 | tf_op jit(solution)/shard_map/all_gather | solution.py:176
  219.8 7.2 reshape.201
  227.0 7.1 fusion.68
  234.1 12.3 %convert_reduce_fusion.1 = (f32[1024]{0:T(1024)}, bf16[2048,1024]{1,0:T(8,128)(2,1)}, bf16[2048,1024]{1,0:T(8,128)(2,1)S(1)}) fusion(f32[2048,1024]{1,0:T(8,128)S(1)} %fusion.68, f32[1024]{0:T(1024)S(1)} %convert_element_type.129, bf16[2048,1024]{1,0:T(8,128)(2,1)S(1)} %copy-done.25, bf16[1024,1024]{1,0:T(8,128)(2,1)S(1)} %copy-done), kind=kOutput, calls=%fused_computation.53 | convolution fusion | flops 4347395072 | bytes 23076864 | tf_op jit(solution)/shard_map/dot_general | solution.py:19
  248.3 6.7 fusion.69
  256.6 9.4 fusion.70
  269.9 57.0 %reduce-scatter.12.cloned.1.call-done = f32[512,1024]{1,0:T(8,128)} async-done(((f32[2048,1024]{1,0:T(8,128)}), f32[512,1024]{1,0:T(8,128)}) %reduce-scatter.12.cloned.1.call-update) | async-done | bytes 2097168 | tf_op jit(solution)/shard_map/reduce_scatter | solution.py:183
  331.1 70.0 %reduce-scatter.14.cloned.1.call-done = f32[512,1024]{1,0:T(8,128)} async-done(((f32[2048,1024]{1,0:T(8,128)}), f32[512,1024]{1,0:T(8,128)}) %reduce-scatter.14.cloned.1.call-update) | async-done | bytes 2097168 | tf_op jit(solution)/shard_map/reduce_scatter | solution.py:200
  408.4 6.0 multiply_reduce_fusion.3
  414.4 8.7 multiply_reduce_fusion.4
  426.3 34.6 %all-gather.5.cloned.1.call-done = bf16[1024,2,1024]{2,1,0:T(2,128)(2,1)} async-done(((bf16[256,2,1024]{2,1,0:T(2,128)(2,1)}), bf16[1024,2,1024]{2,1,0:T(2,128)(2,1)}) %all-gather.5.cloned.1.call-update) | async-done | bytes 4194320 | tf_op jit(solution)/shard_map/all_gather | solution.py:210
  460.9 7.2 reshape.205
  468.0 4.6 convolution_convert_fusion
  472.6 4.4 reshape_reshape.9
  477.0 4.0 copy.75
  482.2 78.4 %while.28 = (s32[]{:T(128)}, f32[1024,2,4,64]{0,3,2,1:T(8,128)S(1)}, f32[1024,2,4,64]{0,3,2,1:T(8,128)}, bf16[2,512,2,4,64]{1,4,3,2,0:T(8,128)(2,1)}, bf16[2,512...) while((s32[]{:T(128)}, ...), condition=%wide.region_15.16_spmd.clone, body=%wide.region_13.15_spmd.clone.sunk | while | flops 2737827840 | bytes 190431536 | solution.py:99
  483.6 3.8 fusion.132
  487.4 4.5 bitcast_add_fusion.5
  491.9 9.6 multiply_reduce_fusion.14
  501.5 10.4 multiply_convert_fusion.6
  511.9 7.2 fusion.133
  522.0 3.8 fusion.132
  525.8 5.7 bitcast_add_fusion.5
  531.5 9.6 multiply_reduce_fusion.14
  541.1 10.4 multiply_convert_fusion.6
  551.5 7.2 fusion.133
  580.8 5.7 convolution_bitcast_fusion
  586.6 10.5 fusion.73
  598.7 5.4 fusion.71
  604.3 10.0 fusion.72
  614.4 7.2 reshape.208
  621.7 4.7 copy.79
  626.4 8.4 fusion.42
  635.0 23.5 %reduce-scatter.16.cloned.1.call-done = f32[512,1024]{1,0:T(8,128)} async-done(((f32[2048,1024]{1,0:T(8,128)}), f32[512,1024]{1,0:T(8,128)}) %reduce-scatter.16.cloned.1.call-update) | async-done | bytes 2097168 | tf_op jit(solution)/shard_map/reduce_scatter | solution.py:228
  661.0 4.7 multiply_reduce_fusion.5
  665.8 11.2 %psum.42 = bf16[2,6144]{1,0:T(2,128)(2,1)S(1)} all-reduce(f32[2,6144]{1,0:T(2,128)S(1)} %bitcast.154), channel_id=1, replica_groups=mesh['dp'=8,'tensor'=4] {'tensor'}, use_global_device_ids=true, to_apply=%region_25.26 | all-reduce | flops 12288 | bytes 73728 | tf_op jit(solution)/shard_map/psum | solution.py:247
  677.0 3.7 fusion.56
  682.6 3.7 mul.285
  687.2 63.0 %reduce-scatter.26.cloned.1.call-done = f32[128,1024]{1,0:T(8,128)} async-done(((f32[1024,1024]{1,0:T(8,128)}), f32[128,1024]{1,0:T(8,128)}) %reduce-scatter.26.cloned.1.call-update) | async-done | bytes 524304 | tf_op jit(solution)/shard_map/reduce_scatter | solution.py:205
  752.6 5.6 convert_reduce_fusion.2
  758.3 59.0 %reduce-scatter.22.cloned.1.call-done = f32[128,256]{1,0:T(8,128)} async-done(((f32[1024,256]{1,0:T(8,128)}), f32[128,256]{1,0:T(8,128)}) %reduce-scatter.22.cloned.1.call-update) | async-done | bytes 131088 | tf_op jit(solution)/shard_map/reduce_scatter | solution.py:256
  821.0 37.2 %all-reduce = (f32[1536]{0:T(1024)}, f32[2,256]{1,0:T(2,128)}, f32[1024]{0:T(1024)}, f32[1024]{0:T(1024)}, f32[1024]{0:T(1024)}) all-reduce(f32[1536]{0:T(1024)S(1)} %convert_reduce_fusion.6, f32[2,256]{1,0:T(2,128)S(1)} %pad_maximum_fusion, f32[1024]{0:T(1024)S(1)} %convert_reduce_fusion.2, ...), channel_id=1, replica_groups=mesh['dp'=8,'tensor'=4] {'dp'}, use_global_device_ids=true, to_apply=%region_28.29 | all-reduce | flops 5120 | bytes 40960 | tf_op jit(solution)/shard_map/psum | solution.py:258
  858.2 5.1 multiply_add_fusion
  863.4 8.7 fusion.55
  872.0 37.1 %reduce-scatter.24.cloned.1.call-done = f32[128,1024]{1,0:T(8,128)} async-done(((f32[1024,1024]{1,0:T(8,128)}), f32[128,1024]{1,0:T(8,128)}) %reduce-scatter.24.cloned.1.call-update) | async-done | bytes 524304 | tf_op jit(solution)/shard_map/reduce_scatter | solution.py:204
  909.1 79.2 %reduce-scatter.20.cloned.1.call-done = f32[128,3,256]{2,0,1:T(8,128)} async-done(((f32[1024,3,256]{2,0,1:T(8,128)}), f32[128,3,256]{2,0,1:T(8,128)}) %reduce-scatter.20.cloned.1.call-update) | async-done | bytes 393232 | tf_op jit(solution)/shard_map/reduce_scatter | solution.py:255
  988.4 121.8 %reduce-scatter.18.cloned.1.call-done = f32[128,1536]{1,0:T(8,128)} async-done(((f32[1024,1536]{1,0:T(8,128)}), f32[128,1536]{1,0:T(8,128)}) %reduce-scatter.18.cloned.1.call-update) | async-done | bytes 786448 | tf_op jit(solution)/shard_map/reduce_scatter | solution.py:254
  (227 shorter events, 102.3 us)
Async XLA Ops:
  7.2 226.9 %copy-start = (bf16[1024,1024]{1,0:T(8,128)(2,1)S(1)}, bf16[1024,1024]{1,0:T(8,128)(2,1)}, u32[]{:S(2)}) copy-start(bf16[1024,1024]{1,0:T(8,128)(2,1)} %param.27) | copy-start | bytes 6291460
  7.2 163.5 %reduce-scatter.10.cloned.1.call-start = ((), (), s32[]{:S(2)}) async-start(), calls=%async_computation.9 | async-start | bytes 10485760 | tf_op jit(solution)/shard_map/reduce_scatter | solution.py:164
  14.5 6.6 copy-start.6
  28.6 12.8 %copy-start.26 = (f32[1024,2]{1,0:T(8,128)}, f32[1024,2]{1,0:T(8,128)S(1)}, u32[]{:S(2)}) copy-start(f32[1024,2]{1,0:T(8,128)S(1)} %add_rsqrt_fusion) | copy-start | bytes 24580
  31.4 10.0 copy-start.29
  31.4 10.0 copy-start.28
  41.4 3.5 copy-start.15
  45.1 2.3 copy-start.49
  51.5 2.9 copy-start.18
  60.4 3.5 copy-start.10
  60.4 3.5 copy-start.22
  72.8 3.5 copy-start.10
  72.8 3.5 copy-start.22
  81.6 14.5 %copy-start.31 = (f32[2,2,4,512]{3,2,1,0:T(4,128)}, f32[2,2,4,512]{3,2,1,0:T(4,128)S(1)}, u32[]{:S(2)}) copy-start(f32[2,2,4,512]{3,2,1,0:T(4,128)S(1)} %get-tuple-element.441) | copy-start | bytes 98308
  96.2 123.7 %all-gather.3.cloned.1.call-start = ((), (), s32[]{:S(2)}) async-start(), calls=%async_computation.10 | async-start | bytes 5242880 | tf_op jit(solution)/shard_map/all_gather | solution.py:176
  96.2 8.6 copy-start.46
  96.2 8.6 copy-start.41
  96.2 8.6 copy-start.42
  96.2 8.6 copy-start.43
  181.1 1.6 copy-start.7
  181.1 4.6 copy-start.47
  181.1 4.6 copy-start.40
  185.2 141.7 %reduce-scatter.12.cloned.1.call-start = ((), (), s32[]{:S(2)}) async-start(), calls=%async_computation.11 | async-start | bytes 10485760 | tf_op jit(solution)/shard_map/reduce_scatter | solution.py:183
  185.7 10.8 copy-start.33
  227.0 7.1 copy-start.25
  246.4 2.0 copy-start.51
  255.0 1.6 copy-start.50
  255.0 146.1 %reduce-scatter.14.cloned.1.call-start = ((), (), s32[]{:S(2)}) async-start(), calls=%async_computation.12 | async-start | bytes 10485760 | tf_op jit(solution)/shard_map/reduce_scatter | solution.py:200
  266.0 194.8 %all-gather.5.cloned.1.call-start = ((), (), s32[]{:S(2)}) async-start(), calls=%async_computation.13 | async-start | bytes 5242880 | tf_op jit(solution)/shard_map/all_gather | solution.py:210
  331.1 77.4 %copy-start.8 = (f32[256,2,1024]{2,1,0:T(2,128)S(1)}, f32[256,2,1024]{2,1,0:T(2,128)}, u32[]{:S(2)}) copy-start(f32[256,2,1024]{2,1,0:T(2,128)} %copy-done.7) | copy-start | bytes 6291460
  408.4 6.0 copy-start.12
  408.4 6.0 copy-start.14
  408.4 6.0 copy-start.34
  426.2 232.2 %reduce-scatter.16.cloned.1.call-start = ((), (), s32[]{:S(2)}) async-start(), calls=%async_computation.14 | async-start | bytes 10485760 | tf_op jit(solution)/shard_map/reduce_scatter | solution.py:228
  472.6 9.6 copy-start.32
  483.6 3.9 copy-start.9
  511.9 7.2 copy-start.2
  511.9 7.2 copy-start.5
  519.1 1.8 copy-start.4
  522.0 3.8 copy-start.9
  551.5 7.2 copy-start.2
  551.5 7.2 copy-start.5
  558.7 1.8 copy-start.4
  569.7 7.9 copy-start.21
  577.5 1.5 copy-start.24
  577.5 3.3 copy-start.27
  579.1 1.7 copy-start.19
  586.6 163.6 %reduce-scatter.26.cloned.1.call-start = ((), (), s32[]{:S(2)}) async-start(), calls=%async_computation.19 | async-start | bytes 4718592 | tf_op jit(solution)/shard_map/reduce_scatter | solution.py:205
  597.2 220.1 %reduce-scatter.22.cloned.1.call-start = ((), (), s32[]{:S(2)}) async-start(), calls=%async_computation.17 | async-start | bytes 1179648 | tf_op jit(solution)/shard_map/reduce_scatter | solution.py:256
  604.1 305.0 %reduce-scatter.24.cloned.1.call-start = ((), (), s32[]{:S(2)}) async-start(), calls=%async_computation.18 | async-start | bytes 4718592 | tf_op jit(solution)/shard_map/reduce_scatter | solution.py:204
  614.4 374.0 %reduce-scatter.20.cloned.1.call-start = ((), (), s32[]{:S(2)}) async-start(), calls=%async_computation.16 | async-start | bytes 3538944 | tf_op jit(solution)/shard_map/reduce_scatter | solution.py:255
  626.4 8.5 copy-start.38
  626.4 8.5 copy-start.36
  626.4 8.5 copy-start.39
  626.4 8.5 copy-start.37
  634.8 26.2 %copy-start.30 = (f32[2,1024]{1,0:T(2,128)S(1)}, f32[2,1024]{1,0:T(2,128)}, u32[]{:S(2)}) copy-start(f32[2,1024]{1,0:T(2,128)} %copy-done.29) | copy-start | bytes 24580
  634.8 475.3 %reduce-scatter.18.cloned.1.call-start = ((), (), s32[]{:S(2)}) async-start(), calls=%async_computation.15 | async-start | bytes 7077888 | tf_op jit(solution)/shard_map/reduce_scatter | solution.py:254
  635.0 42.1 %copy-start.35 = (bf16[2,1024]{1,0:T(2,128)(2,1)S(1)}, bf16[2,1024]{1,0:T(2,128)(2,1)}, u32[]{:S(2)}) copy-start(bf16[2,1024]{1,0:T(2,128)(2,1)} %param.18) | copy-start | bytes 12292
  660.9 19.8 %copy-start.13 = (f32[256,2,1024]{2,1,0:T(2,128)}, f32[256,2,1024]{2,1,0:T(2,128)S(1)}, u32[]{:S(2)}) copy-start(f32[256,2,1024]{2,1,0:T(2,128)S(1)} %reshape.206) | copy-start | bytes 6291460
  680.8 71.4 %copy-start.16 = (bf16[2,512,2,4,64]{1,4,3,2,0:T(8,128)(2,1)S(1)}, bf16[2,512,2,4,64]{1,4,3,2,0:T(8,128)(2,1)}, u32[]{:S(2)}) copy-start(bf16[2,512,2,4,64]{1,4,3,2,0:T(8,128)(2,1)} %get-tuple-element.97) | copy-start | bytes 3145732
  752.4 66.5 %copy-start.17 = (f32[512,1024]{1,0:T(8,128)S(1)}, f32[512,1024]{1,0:T(8,128)}, u32[]{:S(2)}) copy-start(f32[512,1024]{1,0:T(8,128)} %mul.285) | copy-start | bytes 6291460
  752.6 68.4 %copy-start.44 = (f32[1024]{0:T(1024)S(1)}, f32[1024]{0:T(1024)}, u32[]{:S(2)}) copy-start(f32[1024]{0:T(1024)} %get-tuple-element.283) | copy-start | bytes 12292
  752.6 68.4 %copy-start.45 = (f32[1024]{0:T(1024)S(1)}, f32[1024]{0:T(1024)}, u32[]{:S(2)}) copy-start(f32[1024]{0:T(1024)} %get-tuple-element.285) | copy-start | bytes 12292
  858.2 251.9 %copy-start.1 = (bf16[1024,1024]{1,0:T(8,128)(2,1)S(1)}, bf16[1024,1024]{1,0:T(8,128)(2,1)}, u32[]{:S(2)}) copy-start(bf16[1024,1024]{1,0:T(8,128)(2,1)} %param.27) | copy-start | bytes 6291460
  (7 other events, 7.5 us)
Sparse Core Ops, SparseCore 0:
  96.3 74.3 reduce-scatter.9
  185.3 34.4 all-gather.2
  255.1 71.6 reduce-scatter.11
  329.3 71.7 reduce-scatter.13
  426.4 34.4 all-gather.4
  586.7 71.6 reduce-scatter.15
  662.1 88.0 reduce-scatter.25
  754.0 63.2 reduce-scatter.21
  821.5 87.6 reduce-scatter.23
  913.6 74.7 reduce-scatter.19
  992.9 117.1 reduce-scatter.17
where the time goes:
time: 1120 us
  waiting for transfers between devices  627 us (56%)
  matrix products  179 us (16%)
  other arithmetic  129 us (12%)
  local copies, waits for them, and re-layouts  117 us (10%)
  blocking collectives  48.4 us (4%)
  between operations  15 us (1%)
    reduce_scatter x1, waiting for transfers between devices, shards(): lax.psum_scatter(grad_mod_weight, 'dp', scatter_dimension=0, tiled=True)  122 us
    reduce_scatter x1, waiting for transfers between devices, shards(): lax.psum_scatter(grad_qkv, 'dp', scatter_dimension=0, tiled=True)  79.2 us
    reduce_scatter x1, waiting for transfers between devices, shards(): lax.psum_scatter(contract_cols(grad_pre, up_weight), 'tensor', scatter_di...  70 us
    reduce_scatter x1, waiting for transfers between devices, shards(): lax.psum_scatter(jnp.dot(mixed_flat, proj_weight, preferred_element_type=...  65.9 us
    reduce_scatter x1, waiting for transfers between devices, shards(): lax.psum_scatter(grad_down_t, 'dp', scatter_dimension=0, tiled=True)  63 us
    reduce_scatter x1, waiting for transfers between devices, shards(): lax.psum_scatter(grad_proj_t, 'dp', scatter_dimension=0, tiled=True)  59 us
    reduce_scatter x1, waiting for transfers between devices, shards(): lax.psum_scatter(jnp.dot(hidden_low, down_weight, preferred_element_type=...  57 us
    dot_general x5, matrix products, contract_cols(): lax.dot_general(left, right, (((1,), (1,)), ((), ())), preferred_element_...  40.7 us
  transfers between devices with their start and end apart: 11, of which 11 were waited for; matrix products, arithmetic and copies ran while one was open for 12% of the time, Pallas kernels for 0%

commit v1 on v0

v1 whole, which is shorter than its diff:
```python
import jax
import jax.numpy as jnp
from jax import lax
from jax.sharding import PartitionSpec as P

HEAD_DIM = 64
EPS = 1e-06
BF = jnp.bfloat16
F32 = jnp.float32


def dot(left, right, dims=((1,), (0,))):
    return lax.dot_general(left, right, (dims, ((), ())), preferred_element_type=F32)


ROWS = ((0,), (0,))
COLS = ((1,), (1,))


def swap(value, axis, bit):
    pairs = [(i, i ^ bit) for i in range(lax.axis_size(axis))]
    return lax.ppermute(value, axis, pairs)


def normalize(values):
    centre = values - jnp.mean(values, axis=-1, keepdims=True)
    inverse = lax.rsqrt(jnp.mean(centre * centre, axis=-1, keepdims=True) + EPS)
    return centre * inverse, inverse


def norm_back(grad, normed, inverse):
    return inverse * (
        grad
        - jnp.mean(grad, axis=-1, keepdims=True)
        - normed * jnp.mean(grad * normed, axis=-1, keepdims=True)
    )


def gelu_pair(v):
    root = 0.7978845608028654
    inner = jnp.tanh(root * (v + 0.044715 * (v * v * v)))
    half = 0.5 * (1.0 + inner)
    slope = half + 0.5 * v * (1.0 - inner * inner) * (root * (1.0 + 3 * 0.044715 * (v * v)))
    return v * half, slope


def attend(query, key, value):
    seq, cols = query.shape
    heads = cols // HEAD_DIM
    mixed, totals = [], []
    for h in range(heads):
        part = slice(h * HEAD_DIM, (h + 1) * HEAD_DIM)
        scores = dot(query[:, part], key[:, part], COLS) * HEAD_DIM**-0.5
        largest = jnp.max(scores, axis=-1, keepdims=True)
        powers = jnp.exp(scores - largest)
        total = jnp.sum(powers, axis=-1, keepdims=True)
        mixed.append(dot((powers / total).astype(BF), value[:, part]).astype(BF))
        totals.append(largest + jnp.log(total))
    return jnp.concatenate(mixed, 1), jnp.concatenate(totals, 1)


def attend_back(query, key, value, log_total, grad_mixed):
    scale = HEAD_DIM**-0.5
    out = ([], [], [])
    for h in range(query.shape[1] // HEAD_DIM):
        part = slice(h * HEAD_DIM, (h + 1) * HEAD_DIM)
        q, k, v, g = query[:, part], key[:, part], value[:, part], grad_mixed[:, part]
        probs = jnp.exp(dot(q, k, COLS) * scale - log_total[:, h : h + 1])
        grad_probs = dot(g, v, COLS)
        inner = jnp.sum(probs * grad_probs, axis=-1, keepdims=True)
        grad_scores = (probs * (grad_probs - inner)).astype(BF)
        out[0].append((dot(grad_scores, k) * scale).astype(BF))
        out[1].append((dot(grad_scores, q, ROWS) * scale).astype(BF))
        out[2].append(dot(probs.astype(BF), g, ROWS).astype(BF))
    return [jnp.concatenate(o, 1) for o in out]


def quarters(values, place, order):
    rows = values.shape[0] // 4
    return jnp.concatenate(
        [lax.dynamic_slice_in_dim(values, (place ^ k) * rows, rows, 0) for k in order], 0
    )


def token_scatter(partial, place):
    rows = partial.shape[0] // 4
    kept = quarters(partial, place, (2, 0)) + swap(quarters(partial, place, (3, 1)), "tensor", 1)
    return kept[rows:] + swap(kept[:rows].astype(BF), "tensor", 2).astype(F32)


def pieces(own):
    far = swap(own, "tensor", 2)
    return own, far, swap(own, "tensor", 1), swap(far, "tensor", 1)


def halve(value, bit):
    mine = (lax.axis_index("dp") // bit) % 2
    half = value.shape[0] // 2
    keep = lax.dynamic_slice_in_dim(value, mine * half, half, 0)
    send = lax.dynamic_slice_in_dim(value, (1 - mine) * half, half, 0)
    return keep + swap(send.astype(BF), "dp", bit).astype(F32)


def dp_scatter(value):
    size = lax.axis_size("dp")
    rows = value.shape[0] // size
    bits = [1 << i for i in range(size.bit_length() - 1)]
    shape = (2,) * len(bits) + (rows,) + value.shape[1:]
    order = tuple(reversed(range(len(bits)))) + tuple(range(len(bits), len(shape)))
    value = jnp.transpose(value.reshape(shape), order).reshape(value.shape)
    for bit in bits:
        value = halve(value, bit)
    return value


def shards(
    tokens,
    condition,
    modulation_weight,
    modulation_bias,
    qkv_weight,
    qv_bias,
    proj_weight,
    proj_bias,
    up_weight,
    up_bias,
    down_weight,
    down_bias,
    cotangent,
):
    seq, lats, width = tokens.shape
    place = lax.axis_index("tensor")
    quarter = seq // 4
    mod_cols = modulation_weight.shape[1] // 4
    proj = pieces(proj_weight)
    cond = condition.astype(F32)
    silu_low = jax.nn.silu(cond).astype(BF)
    modulation = (dot(silu_low, modulation_weight) + modulation_bias.astype(F32)).reshape(
        lats, 6, width
    )
    qkv_flat = qkv_weight.reshape(width, -1)
    heads = qkv_weight.shape[2]
    qv_float = qv_bias.astype(F32)
    span = range(lats)
    tok = [tokens[:, l] for l in span]
    cot = [cotangent[:, l] for l in span]
    here = lambda value: lax.dynamic_slice_in_dim(value, place * quarter, quarter, 0)
    row = lambda l, i: modulation[l, i : i + 1]

    attend_in, query, key, value = [], [], [], []
    for l in span:
        normed, _ = normalize(tok[l].astype(F32))
        attend_in.append((normed * (1.0 + row(l, 1)) + row(l, 0)).astype(BF))
        projected = dot(attend_in[l], qkv_flat)
        query.append((projected[:, :heads] + qv_float[0]).astype(BF))
        key.append(projected[:, heads : 2 * heads].astype(BF))
        value.append((projected[:, 2 * heads :] + qv_float[1]).astype(BF))

    mixed, log_total, mixed_all = [], [], []
    for l in span:
        m, t = attend(query[l], key[l], value[l])
        mixed.append(m)
        log_total.append(t)
        mixed_all.append(pieces(m))

    update, mlp_in, hidden, grad_pre, grad_mlp, mlp_sum, grad_mlp_in = [], [], [], [], [], [], []
    for l in span:
        u = sum(dot(m, p) for m, p in zip(mixed_all[l], proj)) + proj_bias.astype(F32)
        update.append(here(u))
        stream = tok[l].astype(F32) + row(l, 2) * u
        normed, _ = normalize(stream)
        mlp_in.append((normed * (1.0 + row(l, 4)) + row(l, 3)).astype(BF))
        act, slope = gelu_pair(dot(mlp_in[l], up_weight) + up_bias.astype(F32))
        hidden.append(act.astype(BF))
        mlp_sum.append(token_scatter(dot(hidden[l], down_weight), place))
        grad_mlp.append((row(l, 5) * cot[l].astype(F32)).astype(BF))
        grad_pre.append((dot(grad_mlp[l], down_weight, COLS) * slope).astype(BF))
        grad_mlp_in.append(token_scatter(dot(grad_pre[l], up_weight, COLS), place))

    grad_up = sum(dot(mlp_in[l], grad_pre[l], ROWS) for l in span)
    grad_down = sum(dot(grad_mlp[l], hidden[l], ROWS) for l in span)
    row_sum = lambda values: sum(jnp.sum(v, axis=0, dtype=F32) for v in values)
    up_shard = dp_scatter(grad_up)
    down_shard = dp_scatter(grad_down).T

    grad_stream, grad_update, stats, outs = [], [], [], []
    for l in span:
        stream = here(tok[l]).astype(F32) + row(l, 2) * update[l]
        normed, inverse = normalize(stream)
        cot_here = here(cot[l]).astype(F32)
        g = cot_here + norm_back(grad_mlp_in[l] * (1.0 + row(l, 4)), normed, inverse)
        grad_stream.append(g)
        grad_update.append(pieces((row(l, 2) * g).astype(BF)))
        mlp_update = mlp_sum[l] + down_bias.astype(F32)
        outs.append((stream + row(l, 5) * mlp_update).astype(BF))
        total = lambda v: jnp.sum(v, axis=0)
        stats.append(
            [
                total(g * update[l]),
                total(grad_mlp_in[l]),
                total(grad_mlp_in[l] * normed),
                total(cot_here * mlp_update),
            ]
        )

    grad_qkv_low, grad_proj, grad_tokens, mod_part = [], [], [], []
    for l in span:
        near = grad_update[l]
        whole = jnp.zeros((seq, width), BF)
        for k, piece in zip((0, 2, 1, 3), near):
            whole = lax.dynamic_update_slice_in_dim(whole, piece, (place ^ k) * quarter, 0)
        grad_proj.append(dot(whole, mixed[l], ROWS))
        grad_mixed = dot(whole, proj_weight, COLS).astype(BF)
        grads = attend_back(query[l], key[l], value[l], log_total[l], grad_mixed)
        grad_qkv_low.append(jnp.concatenate(grads, 1))
        grad_in = token_scatter(dot(grad_qkv_low[l], qkv_flat, COLS), place)
        normed, inverse = normalize(here(tok[l]).astype(F32))
        grad_tokens.append(
            grad_stream[l] + norm_back(grad_in * (1.0 + row(l, 1)), normed, inverse)
        )
        mod_part.append(jnp.stack([jnp.sum(grad_in, axis=0), jnp.sum(grad_in * normed, axis=0)] + stats[l]))

    grad_qkv = sum(dot(attend_in[l], grad_qkv_low[l], ROWS) for l in span)
    qkv_shard = dp_scatter(grad_qkv).reshape(-1, 3, heads)
    proj_shard = dp_scatter(sum(grad_proj)).T

    mod = jnp.stack(mod_part).reshape(lats, -1)
    mod = mod + swap(mod, "tensor", 1)
    mod = mod + swap(mod, "tensor", 2)
    grad_modulation = mod.astype(BF)
    own_cols = lax.dynamic_slice_in_dim(grad_modulation, place * mod_cols, mod_cols, 1)
    own_weight = lax.dynamic_slice_in_dim(modulation_weight, place * mod_cols, mod_cols, 1)
    grad_silu = dot(own_cols, own_weight, COLS)
    grad_silu = grad_silu + swap(grad_silu, "tensor", 1)
    grad_silu = grad_silu + swap(grad_silu, "tensor", 2)
    grad_condition = jax.vjp(jax.nn.silu, cond)[1](grad_silu)[0]

    qkv_sum = row_sum(grad_qkv_low)
    biases = jnp.concatenate(
        [
            row_sum(grad_pre),
            row_sum(grad_mlp),
            row_sum([p for l in span for p in grad_update[l]]),
            qkv_sum[:heads],
            qkv_sum[2 * heads :],
        ]
    )
    gathered = jnp.concatenate([silu_low.astype(F32), own_cols.astype(F32)], 1)
    size = lax.axis_size("dp")
    index = lax.axis_index("dp")
    for bit in [1 << i for i in range(size.bit_length() - 1)]:
        other = swap(jnp.concatenate([gathered.reshape(-1), biases]), "dp", bit)
        theirs = other[: gathered.size].reshape(gathered.shape)
        biases = biases + other[gathered.size :]
        low = (index // bit) % 2 == 0
        gathered = jnp.concatenate(
            [jnp.where(low, gathered, theirs), jnp.where(low, theirs, gathered)], 0
        )
    all_silu = gathered[:, :width].astype(BF)
    all_cols = gathered[:, width:].astype(BF)
    mod_rows = width // size
    my_silu = lax.dynamic_slice_in_dim(all_silu, index * mod_rows, mod_rows, 1)
    mod_shard = dot(my_silu, all_cols, ROWS)
    mod_bias_sum = jnp.sum(all_cols, axis=0, dtype=F32)
    ff = up_weight.shape[1]
    ends = [ff, ff + width, ff + 2 * width, ff + 2 * width + heads]
    up_bias_sum, down_bias_sum, proj_bias_sum, q_sum, v_sum = jnp.split(biases, ends)
    return (
        jnp.stack(outs, 1),
        jnp.stack(grad_tokens, 1),
        grad_condition,
        mod_shard,
        mod_bias_sum,
        qkv_shard,
        jnp.stack([q_sum, v_sum]),
        proj_shard,
        proj_bias_sum,
        up_shard,
        up_bias_sum,
        down_shard,
        down_bias_sum,
    )


def solution(mesh):
    in_specs = (
        P(None, "dp", None),
        P("dp", None),
        P(),
        P(),
        P(None, None, "tensor"),
        P(None, "tensor"),
        P("tensor", None),
        P(),
        P(None, "tensor"),
        P("tensor"),
        P("tensor", None),
        P(),
        P(None, "dp", None),
    )
    out_specs = (
        P("tensor", "dp", None),
        P("tensor", "dp", None),
        P("dp", None),
        P("dp", "tensor"),
        P("tensor"),
        P("dp", None, "tensor"),
        P(None, "tensor"),
        P("tensor", "dp"),
        P(),
        P("dp", "tensor"),
        P("tensor"),
        P("tensor", "dp"),
        P(),
    )
    return jax.shard_map(shards, mesh=mesh, in_specs=in_specs, out_specs=out_specs, check_vma=False)
```

time: 1120 us -> 608 us (0.54)
  waiting for transfers between devices: 627 us -> 134 us
  blocking collectives: 48.4 us -> 0 us
  starting transfers between devices: 1.13 us -> 42.3 us
  other arithmetic: 129 us -> 107 us
  local copies, waits for them, and re-layouts: 117 us -> 132 us
  between operations: 15 us -> 3.58 us
    reduce_scatter x9 -> x0, waiting for transfers between devices: 576 us -> none  [the longest x1 122 us: shards(): lax.psum_scatter(grad_mod_weight, 'dp', scatter_dimension=0, tiled=True)]
    ppermute x0 -> x46, waiting for transfers between devices: none -> 134 us  [swap(): return lax.ppermute(value, axis, pairs)]
    all_gather x2 -> x0, waiting for transfers between devices: 50.5 us -> none  [the longest x1 34.6 us: shards(): lax.all_gather(update_here, 'tensor', axis=0, tiled=True)]
    psum x2 -> x0, blocking collectives: 48.4 us -> none  [the longest x1 37.2 us: shards(): lax.psum((grad_mod_bias, grad_qv_bias, grad_proj_bias), 'dp')]
    unnamed x99 -> x301, local copies, waits for them, and re-layouts: 20.8 us -> 66.2 us
    ppermute x0 -> x46, starting transfers between devices: none -> 42.3 us  [swap(): return lax.ppermute(value, axis, pairs)]
    reshape x9 -> x10, local copies, waits for them, and re-layouts: 40.6 us -> 9.07 us  [the longest x3 8.87 us: dp_scatter(): value = jnp.transpose(value.reshape(shape), order).reshape(value.shape)]
    another operation x19 -> x4, local copies, waits for them, and re-layouts: 23.7 us -> 1.92 us  [the longest x5 11.5 us: shards(): jnp.stack([grad_query.reshape(rows, -1), grad_key.reshape(rows, -1), grad...]
  transfers between devices with their start and end apart: 11 -> 46, of which waited for: 11 -> 18; matrix products, arithmetic and copies ran while one was open for 12% -> 47% of each run, Pallas kernels for 0% -> 0%
where the time goes in v1:
time: 608 us; the launch traced here: 601 us
  matrix products  182 us (30%)
  waiting for transfers between devices  134 us (22%)
  local copies, waits for them, and re-layouts  132 us (22%)
  other arithmetic  107 us (18%)
  starting transfers between devices  42.3 us (7%)
    dot_general x81, matrix products, dot(): lax.dot_general(left, right, (dims, ((), ())), preferred_element_type=F32)  182 us
    ppermute x46, waiting for transfers between devices, swap(): return lax.ppermute(value, axis, pairs)  134 us
    unnamed x301, local copies, waits for them, and re-layouts  66.2 us
    ppermute x46, starting transfers between devices, swap(): return lax.ppermute(value, axis, pairs)  42.3 us
    convert_element_type x8, other arithmetic, attend_back(): grad_scores = (probs * (grad_probs - inner)).astype(BF)  18.1 us
    reduce_sum x11, other arithmetic, shards(): jnp.sum(v, axis=0, dtype=F32)  14.5 us
    dynamic_update_slice x8, local copies, waits for them, and re-layouts, shards(): lax.dynamic_update_slice_in_dim(whole, piece, (place ^ k) * quarter, 0)  13.6 us
  transfers between devices with their start and end apart: 46, of which 18 were waited for; matrix products, arithmetic and copies ran while one was open for 47% of the time, Pallas kernels for 0%

profile of v1, /device:TPU:0, one launch (start us, length us, event | category | flops | bytes accessed | tf_op | source)
XLA Modules:
  0.0 600.6 jit_solution(7178351049425870258)
XLA Ops:
  0.7 10.2 %fusion.378 = (bf16[1024,1,1024]{2,1,0:T(2,128)(2,1)}, bf16[1024,1,1024]{2,1,0:T(2,128)(2,1)}) fusion(bf16[1024,2,1024]{2,1,0:T(2,128)(2,1)} %param.13), kind=kLoop, calls=%fused_computation.617 | loop fusion | bytes 8388608 | tf_op jit(solution)/shard_map/slice | solution.py:145
  10.8 10.7 %copy.140 = bf16[1024,1,1024]{0,2,1:T(8,128)(2,1)} copy(bf16[1024,1,1024]{2,1,0:T(2,128)(2,1)} %get-tuple-element.107) | data formatting | bytes 4194304
  25.7 6.3 %convolution_add_fusion = f32[2,6144]{1,0:T(2,128)S(1)} fusion(bf16[1024,6144]{1,0:T(8,128)(2,1)} %param.15, f32[6144]{0:T(1024)S(1)} %convert_element_type.470, bf16[2,1024]{1,0:T(2,128)(2,1)S(1)} %copy-done.105), kind=kOutput, calls=%fused_computation | convolution fusion | flops 25190400 | bytes 12660736 | tf_op jit(solution)/shard_map/dot_general | solution.py:13
  32.8 2.6 copy.97
  35.4 10.8 %copy.139 = bf16[1024,1,1024]{0,2,1:T(8,128)(2,1)} copy(bf16[1024,1,1024]{2,1,0:T(2,128)(2,1)} %get-tuple-element.106) | data formatting | bytes 4194304
  66.9 3.0 collective-permute-start.8
  83.3 2.9 fusion.366
  101.3 10.2 %fusion.377 = (bf16[1024,1,1024]{2,1,0:T(2,128)(2,1)}, bf16[1024,1,1024]{2,1,0:T(2,128)(2,1)}) fusion(bf16[1024,2,1024]{2,1,0:T(2,128)(2,1)} %param.25), kind=kLoop, calls=%fused_computation.616 | loop fusion | bytes 8388608 | tf_op jit(solution)/shard_map/slice | solution.py:146
  111.5 10.6 %copy.141 = bf16[1024,1,1024]{0,2,1:T(8,128)(2,1)} copy(bf16[1024,1,1024]{2,1,0:T(2,128)(2,1)} %get-tuple-element.92) | data formatting | bytes 4194304
  123.4 10.6 %copy.142 = bf16[1024,1,1024]{0,2,1:T(8,128)(2,1)} copy(bf16[1024,1,1024]{2,1,0:T(2,128)(2,1)} %get-tuple-element.93) | data formatting | bytes 4194304
  136.5 2.7 convert_reduce_fusion.3
  139.2 2.7 convert_reduce_fusion.2
  157.3 2.4 fusion.387
  159.8 4.5 fusion.356
  164.3 5.8 convert_reduce_fusion.5
  170.0 4.3 fusion.395
  174.3 4.7 fusion.391
  184.5 2.4 fusion.390
  186.9 7.2 %convert_reduce_fusion.4 = (f32[1024]{0:T(1024)}, bf16[1024,1024]{1,0:T(8,128)(2,1)}) fusion(f32[1024,1024]{1,0:T(8,128)S(1)} %fusion.390, f32[1024]{0:T(1024)S(1)} %copy-done.130, bf16[1024,1024]{1,0:T(8,128)(2,1)S(1)} %copy-done, bf16[1024,1,1024]{0,2,1:T(8,128)(2,1)S(1)} %copy-done.30, f32[1024]{0:T(1024)S(1)} %bitcast.325), kind=kOutput, calls=%fused_computation.61 | convolution fusion | flops 2172648448 | bytes 10498048 | tf_op jit(solution)/shard_map/dot_general | solution.py:13
  194.1 4.6 fusion.370
  198.7 4.7 fusion.371
  203.5 4.5 convolution_add_fusion.1
  208.0 7.2 %copy.129 = f32[2,2,2,128,1024]{3,2,1,0,4:T(2,128)} copy(f32[2,2,2,128,1024]{4,3,0,1,2:T(8,128)} %bitcast.285) | data formatting | bytes 8388608 | tf_op jit(solution)/shard_map/transpose | solution.py:110
  215.2 6.8 %reshape.430 = f32[1024,1024]{0,1:T(8,128)} reshape(f32[2,2,2,128,1024]{3,2,1,0,4:T(2,128)} %copy.129) | data formatting | bytes 8388608 | tf_op jit(solution)/shard_map/reshape | solution.py:110
  222.0 2.7 dynamic-slice_convert_fusion
  226.2 4.7 fusion.393
  245.5 5.5 collective-permute-done.43
  254.6 18.0 %collective-permute-done.40 = bf16[512,1024]{1,0:T(8,128)(2,1)} collective-permute-done((bf16[512,1024]{1,0:T(8,128)(2,1)}, bf16[512,1024]{1,0:T(8,128)(2,1)}, u32[]{:S(2)}, u32[]{:S(2)}) %collective-permute-start.40) | collective-permute-done | bytes 1048608 | tf_op jit(solution)/shard_map/ppermute | solution.py:22
  276.2 12.5 %collective-permute-done.41 = bf16[256,1024]{1,0:T(8,128)(2,1)S(1)} collective-permute-done((bf16[256,1024]{1,0:T(8,128)(2,1)S(1)}, bf16[256,1024]{1,0:T(8,128)(2,1)S(1)}, u32[]{:S(2)}, u32[]{:S(2)}) %collective-permute-start.41) | collective-permute-done | bytes 524320 | tf_op jit(solution)/shard_map/ppermute | solution.py:22
  288.7 2.6 collective-permute-start.45
  291.5 11.7 %collective-permute-done.45 = bf16[128,1024]{0,1:T(8,128)(2,1)S(1)} collective-permute-done((bf16[128,1024]{0,1:T(8,128)(2,1)S(1)}, bf16[128,1024]{0,1:T(8,128)(2,1)S(1)}, u32[]{:S(2)}, u32[]{:S(2)}) %collective-permute-start.45) | collective-permute-done | bytes 262176 | tf_op jit(solution)/shard_map/ppermute | solution.py:22
  310.3 9.1 %collective-permute-done.14 = bf16[256,1024]{0,1:T(8,128)(2,1)S(1)} collective-permute-done((bf16[256,1024]{0,1:T(8,128)(2,1)S(1)}, bf16[256,1024]{0,1:T(8,128)(2,1)S(1)}, u32[]{:S(2)}, u32[]{:S(2)}) %collective-permute-start.14) | collective-permute-done | bytes 524320 | tf_op jit(solution)/shard_map/ppermute | solution.py:22
  319.4 11.2 %collective-permute-done.21 = bf16[256,1024]{0,1:T(8,128)(2,1)S(1)} collective-permute-done((bf16[256,1024]{0,1:T(8,128)(2,1)S(1)}, bf16[256,1024]{0,1:T(8,128)(2,1)S(1)}, u32[]{:S(2)}, u32[]{:S(2)}) %collective-permute-start.21) | collective-permute-done | bytes 524320 | tf_op jit(solution)/shard_map/ppermute | solution.py:22
  331.9 10.0 %collective-permute-done.12 = bf16[256,1024]{0,1:T(8,128)(2,1)S(1)} collective-permute-done((bf16[256,1024]{0,1:T(8,128)(2,1)S(1)}, bf16[256,1024]{0,1:T(8,128)(2,1)S(1)}, u32[]{:S(2)}, u32[]{:S(2)}) %collective-permute-start.12) | collective-permute-done | bytes 524320 | tf_op jit(solution)/shard_map/ppermute | solution.py:22
  341.8 9.2 %collective-permute-done.7 = bf16[256,1024]{0,1:T(8,128)(2,1)S(1)} collective-permute-done((bf16[256,1024]{0,1:T(8,128)(2,1)S(1)}, bf16[256,1024]{0,1:T(8,128)(2,1)S(1)}, u32[]{:S(2)}, u32[]{:S(2)}) %collective-permute-start.7) | collective-permute-done | bytes 524320 | tf_op jit(solution)/shard_map/ppermute | solution.py:22
  351.0 3.3 fusion.233
  369.4 8.2 %collective-permute-done.15 = bf16[256,1024]{0,1:T(8,128)(2,1)} collective-permute-done((bf16[256,1024]{0,1:T(8,128)(2,1)}, bf16[256,1024]{0,1:T(8,128)(2,1)}, u32[]{:S(2)}, u32[]{:S(2)}) %collective-permute-start.15) | collective-permute-done | bytes 524320 | tf_op jit(solution)/shard_map/ppermute | solution.py:22
  392.2 3.5 fusion.365
  400.2 3.1 multiply_reduce_fusion.1
  405.5 2.9 multiply_reduce_fusion.3
  408.4 3.3 multiply_convert_fusion.3
  415.0 3.3 multiply_convert_fusion.1
  423.6 2.4 fusion.162
  437.7 5.3 fusion.394
  443.1 3.8 fusion.70
  449.0 3.1 convolution_convert_fusion.1
  452.1 3.3 convolution_add_fusion.3
  462.5 3.4 multiply_reduce_fusion.4
  466.0 3.0 multiply_reduce_fusion.5
  471.1 2.9 multiply_reduce_fusion.7
  474.1 3.5 multiply_convert_fusion.7
  480.8 3.3 multiply_convert_fusion.5
  503.3 3.2 fusion.392
  519.6 5.7 collective-permute-start.38
  525.5 3.6 collective-permute-done.38
  530.9 3.9 collective-permute-done.39
  536.5 8.8 %collective-permute-done.19 = bf16[256,1024]{0,1:T(8,128)(2,1)S(1)} collective-permute-done((bf16[256,1024]{0,1:T(8,128)(2,1)S(1)}, bf16[256,1024]{0,1:T(8,128)(2,1)S(1)}, u32[]{:S(2)}, u32[]{:S(2)}) %collective-permute-start.19) | collective-permute-done | bytes 524320 | tf_op jit(solution)/shard_map/ppermute | solution.py:22
  545.9 9.0 %collective-permute-done.26 = bf16[256,1024]{0,1:T(8,128)(2,1)S(1)} collective-permute-done((bf16[256,1024]{0,1:T(8,128)(2,1)S(1)}, bf16[256,1024]{0,1:T(8,128)(2,1)S(1)}, u32[]{:S(2)}, u32[]{:S(2)}) %collective-permute-start.26) | collective-permute-done | bytes 524320 | tf_op jit(solution)/shard_map/ppermute | solution.py:22
  557.8 2.7 multiply_reduce_fusion.19
  567.0 2.8 fusion.54
  569.8 4.9 collective-permute-done.35
  580.9 2.7 collective-permute-done.31
  590.2 2.8 pad_maximum_fusion.6
  593.1 4.1 copy.131
  (605 shorter events, 241.4 us)
Async XLA Ops:
  0.6 163.6 %copy-start = (bf16[1024,1024]{1,0:T(8,128)(2,1)S(1)}, bf16[1024,1024]{1,0:T(8,128)(2,1)}, u32[]{:S(2)}) copy-start(bf16[1024,1024]{1,0:T(8,128)(2,1)} %param.23) | copy-start | bytes 6291460
  23.5 27.1 %copy-start.112 = (f32[1024]{0:T(1024)}, f32[1024]{0:T(1024)S(1)}, u32[]{:S(2)}) copy-start(f32[1024]{0:T(1024)S(1)} %broadcast_multiply_fusion.1) | copy-start | bytes 12292
  25.7 24.9 %copy-start.133 = (f32[1024]{0:T(1024)}, f32[1024]{0:T(1024)S(1)}, u32[]{:S(2)}) copy-start(f32[1024]{0:T(1024)S(1)} %add_rsqrt_fusion.1) | copy-start | bytes 12292
  32.8 19.9 %copy-start.91 = (f32[1,1,1024]{2,1,0:T(1,128)}, f32[1,1,1024]{2,1,0:T(1,128)S(1)}, u32[]{:S(2)}) copy-start(f32[1,1,1024]{2,1,0:T(1,128)S(1)} %get-tuple-element.141) | copy-start | bytes 12292
  32.8 19.9 %copy-start.126 = (f32[1,1,1024]{2,1,0:T(1,128)}, f32[1,1,1024]{2,1,0:T(1,128)S(1)}, u32[]{:S(2)}) copy-start(f32[1,1,1024]{2,1,0:T(1,128)S(1)} %get-tuple-element.140) | copy-start | bytes 12292
  55.0 24.7 %copy-start.44 = (bf16[1024,256]{0,1:T(8,128)(2,1)}, bf16[1024,256]{0,1:T(8,128)(2,1)S(1)}, u32[]{:S(2)}) copy-start(bf16[1024,256]{0,1:T(8,128)(2,1)S(1)} %get-tuple-element.159) | copy-start | bytes 1572868
  60.4 22.9 %copy-start.73 = (bf16[1024,64]{0,1:T(8,128)(2,1)}, bf16[1024,64]{0,1:T(8,128)(2,1)S(1)}, u32[]{:S(2)}) copy-start(bf16[1024,64]{0,1:T(8,128)(2,1)S(1)} %fusion.214) | copy-start | bytes 393220
  62.1 21.2 %copy-start.75 = (bf16[1024,64]{0,1:T(8,128)(2,1)}, bf16[1024,64]{0,1:T(8,128)(2,1)S(1)}, u32[]{:S(2)}) copy-start(bf16[1024,64]{0,1:T(8,128)(2,1)S(1)} %fusion.213) | copy-start | bytes 393220
  66.9 76.7 %collective-permute-start.8 = (bf16[1024,256]{0,1:T(8,128)(2,1)}, bf16[1024,256]{0,1:T(8,128)(2,1)}, u32[]{:S(2)}, u32[]{:S(2)}) collective-permute-start(bf16[1024,256]{0,1:T(8,128)(2,1)} %pad_maximum_fusion.9), channel_id=1, source_target_pairs={{0,2},{1,3},{2,0},{3,1},{4,6},{5,7},{6,4},{7,5},{8,10},{9,11},{10,... | collective-permute-start | bytes 1572872 | tf_op jit(solution)/shard_map/ppermute | solution.py:22
  69.9 78.1 %collective-permute-start.9 = (bf16[1024,256]{0,1:T(8,128)(2,1)}, bf16[1024,256]{0,1:T(8,128)(2,1)}, u32[]{:S(2)}, u32[]{:S(2)}) collective-permute-start(bf16[1024,256]{0,1:T(8,128)(2,1)} %pad_maximum_fusion.9), channel_id=1, source_target_pairs={{0,1},{1,0},{2,3},{3,2},{4,5},{5,4},{6,7},{7,6},{8,9},{9,8},{10,11... | collective-permute-start | bytes 1572872 | tf_op jit(solution)/shard_map/ppermute | solution.py:22
  69.9 73.9 %collective-permute-start.1 = (bf16[256,1024]{1,0:T(8,128)(2,1)S(1)}, bf16[256,1024]{1,0:T(8,128)(2,1)S(1)}, u32[]{:S(2)}, u32[]{:S(2)}) collective-permute-start(bf16[256,1024]{1,0:T(8,128)(2,1)S(1)} %copy-done.49), channel_id=1, source_target_pairs={{0,2},{1,3},{2,0},{3,1},{4,6},{5,7},{6,4},{7,5},{8,10},{9,11},{10,... | collective-permute-start | bytes 1572872 | tf_op jit(solution)/shard_map/ppermute | solution.py:22
  70.0 78.6 %collective-permute-start.3 = (bf16[256,1024]{1,0:T(8,128)(2,1)S(1)}, bf16[256,1024]{1,0:T(8,128)(2,1)}, u32[]{:S(2)}, u32[]{:S(2)}) collective-permute-start(bf16[256,1024]{1,0:T(8,128)(2,1)S(1)} %copy-done.49), channel_id=1, source_target_pairs={{0,1},{1,0},{2,3},{3,2},{4,5},{5,4},{6,7},{7,6},{8,9},{9,8},{10,11... | collective-permute-start | bytes 1572872 | tf_op jit(solution)/shard_map/ppermute | solution.py:22
  75.6 66.4 %copy-start.65 = (bf16[1024,64]{0,1:T(8,128)(2,1)}, bf16[1024,64]{0,1:T(8,128)(2,1)S(1)}, u32[]{:S(2)}) copy-start(bf16[1024,64]{0,1:T(8,128)(2,1)S(1)} %fusion.218) | copy-start | bytes 393220
  77.3 64.7 %copy-start.67 = (bf16[1024,64]{0,1:T(8,128)(2,1)}, bf16[1024,64]{0,1:T(8,128)(2,1)S(1)}, u32[]{:S(2)}) copy-start(bf16[1024,64]{0,1:T(8,128)(2,1)S(1)} %fusion.217) | copy-start | bytes 393220
  79.0 63.0 %copy-start.69 = (bf16[1024,64]{0,1:T(8,128)(2,1)}, bf16[1024,64]{0,1:T(8,128)(2,1)S(1)}, u32[]{:S(2)}) copy-start(bf16[1024,64]{0,1:T(8,128)(2,1)S(1)} %fusion.216) | copy-start | bytes 393220
  81.6 64.5 %collective-permute-start = (bf16[1024,256]{0,1:T(8,128)(2,1)}, bf16[1024,256]{0,1:T(8,128)(2,1)}, u32[]{:S(2)}, u32[]{:S(2)}) collective-permute-start(bf16[1024,256]{0,1:T(8,128)(2,1)} %pad_maximum_fusion.8), channel_id=1, source_target_pairs={{0,2},{1,3},{2,0},{3,1},{4,6},{5,7},{6,4},{7,5},{8,10},{9,11},{10,... | collective-permute-start | bytes 1572872 | tf_op jit(solution)/shard_map/ppermute | solution.py:22
  143.7 6.8 %collective-permute-start.2 = (bf16[1024,256]{0,1:T(8,128)(2,1)}, bf16[1024,256]{0,1:T(8,128)(2,1)S(1)}, u32[]{:S(2)}, u32[]{:S(2)}) collective-permute-start(bf16[1024,256]{0,1:T(8,128)(2,1)} %pad_maximum_fusion.8), channel_id=1, source_target_pairs={{0,1},{1,0},{2,3},{3,2},{4,5},{5,4},{6,7},{7,6},{8,9},{9,8},{10,11... | collective-permute-start | bytes 1572872 | tf_op jit(solution)/shard_map/ppermute | solution.py:22
  143.8 35.3 %collective-permute-start.10 = (bf16[1024,256]{0,1:T(8,128)(2,1)}, bf16[1024,256]{0,1:T(8,128)(2,1)S(1)}, u32[]{:S(2)}, u32[]{:S(2)}) collective-permute-start(bf16[1024,256]{0,1:T(8,128)(2,1)} %collective-permute-done.8), channel_id=1, source_target_pairs={{0,1},{1,0},{2,3},{3,2},{4,5},{5,4},{6,7},{7,6},{8,9},{9,8},{10,11... | collective-permute-start | bytes 1572872 | tf_op jit(solution)/shard_map/ppermute | solution.py:22
  146.1 6.4 %collective-permute-start.5 = (bf16[256,1024]{1,0:T(8,128)(2,1)S(1)}, bf16[256,1024]{1,0:T(8,128)(2,1)S(1)}, u32[]{:S(2)}, u32[]{:S(2)}) collective-permute-start(bf16[256,1024]{1,0:T(8,128)(2,1)S(1)} %collective-permute-done.1), channel_id=1, source_target_pairs={{0,1},{1,0},{2,3},{3,2},{4,5},{5,4},{6,7},{7,6},{8,9},{9,8},{10,11... | collective-permute-start | bytes 1572872 | tf_op jit(solution)/shard_map/ppermute | solution.py:22
  148.0 4.5 collective-permute-start.4
  224.7 26.3 %collective-permute-start.43 = (bf16[512,1024]{0,1:T(8,128)(2,1)}, bf16[512,1024]{0,1:T(8,128)(2,1)}, u32[]{:S(2)}, u32[]{:S(2)}) collective-permute-start(bf16[512,1024]{0,1:T(8,128)(2,1)} %dynamic-slice_convert_fusion), channel_id=1, source_target_pairs={{0,4},{4,0},{8,12},{12,8},{16,20},{20,16},{24,28},{28,24},{1,5},{5... | collective-permute-start | bytes 3145736 | tf_op jit(solution)/shard_map/ppermute | solution.py:22
  235.1 37.5 %collective-permute-start.40 = (bf16[512,1024]{1,0:T(8,128)(2,1)}, bf16[512,1024]{1,0:T(8,128)(2,1)}, u32[]{:S(2)}, u32[]{:S(2)}) collective-permute-start(bf16[512,1024]{1,0:T(8,128)(2,1)} %dynamic-slice_convert_fusion.1), channel_id=1, source_target_pairs={{0,4},{4,0},{8,12},{12,8},{16,20},{20,16},{24,28},{28,24},{1,5},{5... | collective-permute-start | bytes 3145736 | tf_op jit(solution)/shard_map/ppermute | solution.py:22
  236.8 67.2 %collective-permute-start.13 = (f32[512,1024]{0,1:T(8,128)S(1)}, f32[512,1024]{0,1:T(8,128)S(1)}, u32[]{:S(2)}, u32[]{:S(2)}) collective-permute-start(f32[512,1024]{0,1:T(8,128)S(1)} %pad_maximum_fusion.2), channel_id=1, source_target_pairs={{0,1},{1,0},{2,3},{3,2},{4,5},{5,4},{6,7},{7,6},{8,9},{9,8},{10,11... | collective-permute-start | bytes 6291464 | tf_op jit(solution)/shard_map/ppermute | solution.py:22
  237.7 67.2 %collective-permute-start.20 = (f32[512,1024]{0,1:T(8,128)S(1)}, f32[512,1024]{0,1:T(8,128)S(1)}, u32[]{:S(2)}, u32[]{:S(2)}) collective-permute-start(f32[512,1024]{0,1:T(8,128)S(1)} %pad_maximum_fusion.4), channel_id=1, source_target_pairs={{0,1},{1,0},{2,3},{3,2},{4,5},{5,4},{6,7},{7,6},{8,9},{9,8},{10,11... | collective-permute-start | bytes 6291464 | tf_op jit(solution)/shard_map/ppermute | solution.py:22
  243.0 64.1 %collective-permute-start.11 = (f32[512,1024]{0,1:T(8,128)S(1)}, f32[512,1024]{0,1:T(8,128)S(1)}, u32[]{:S(2)}, u32[]{:S(2)}) collective-permute-start(f32[512,1024]{0,1:T(8,128)S(1)} %pad_maximum_fusion.1), channel_id=1, source_target_pairs={{0,1},{1,0},{2,3},{3,2},{4,5},{5,4},{6,7},{7,6},{8,9},{9,8},{10,11... | collective-permute-start | bytes 6291464 | tf_op jit(solution)/shard_map/ppermute | solution.py:22
  252.7 21.6 %collective-permute-start.44 = (bf16[256,1024]{0,1:T(8,128)(2,1)S(1)}, bf16[256,1024]{0,1:T(8,128)(2,1)S(1)}, u32[]{:S(2)}, u32[]{:S(2)}) collective-permute-start(bf16[256,1024]{0,1:T(8,128)(2,1)S(1)} %dynamic-slice_convert_fusion.3), channel_id=1, source_target_pairs={{0,8},{4,12},{8,0},{12,4},{16,24},{20,28},{24,16},{28,20},{1,9},{5... | collective-permute-start | bytes 1572872 | tf_op jit(solution)/shard_map/ppermute | solution.py:22
  272.6 35.4 %collective-permute-start.6 = (f32[512,1024]{0,1:T(8,128)S(1)}, f32[512,1024]{0,1:T(8,128)S(1)}, u32[]{:S(2)}, u32[]{:S(2)}) collective-permute-start(f32[512,1024]{0,1:T(8,128)S(1)} %pad_maximum_fusion), channel_id=1, source_target_pairs={{0,1},{1,0},{2,3},{3,2},{4,5},{5,4},{6,7},{7,6},{8,9},{9,8},{10,11... | collective-permute-start | bytes 6291464 | tf_op jit(solution)/shard_map/ppermute | solution.py:22
  274.3 14.4 %collective-permute-start.41 = (bf16[256,1024]{1,0:T(8,128)(2,1)S(1)}, bf16[256,1024]{1,0:T(8,128)(2,1)S(1)}, u32[]{:S(2)}, u32[]{:S(2)}) collective-permute-start(bf16[256,1024]{1,0:T(8,128)(2,1)S(1)} %dynamic-slice_convert_fusion.4), channel_id=1, source_target_pairs={{0,8},{4,12},{8,0},{12,4},{16,24},{20,28},{24,16},{28,20},{1,9},{5... | collective-permute-start | bytes 1572872 | tf_op jit(solution)/shard_map/ppermute | solution.py:22
  288.7 14.5 %collective-permute-start.45 = (bf16[128,1024]{0,1:T(8,128)(2,1)S(1)}, bf16[128,1024]{0,1:T(8,128)(2,1)S(1)}, u32[]{:S(2)}, u32[]{:S(2)}) collective-permute-start(bf16[128,1024]{0,1:T(8,128)(2,1)S(1)} %dynamic-slice_convert_fusion.6), channel_id=1, source_target_pairs={{0,16},{4,20},{8,24},{12,28},{16,0},{20,4},{24,8},{28,12},{1,17},{... | collective-permute-start | bytes 786440 | tf_op jit(solution)/shard_map/ppermute | solution.py:22
  303.1 55.1 %collective-permute-start.42 = (bf16[128,1024]{1,0:T(8,128)(2,1)S(1)}, bf16[128,1024]{1,0:T(8,128)(2,1)S(1)}, u32[]{:S(2)}, u32[]{:S(2)}) collective-permute-start(bf16[128,1024]{1,0:T(8,128)(2,1)S(1)} %dynamic-slice_convert_fusion.7), channel_id=1, source_target_pairs={{0,16},{4,20},{8,24},{12,28},{16,0},{20,4},{24,8},{28,12},{1,17},{... | collective-permute-start | bytes 786440 | tf_op jit(solution)/shard_map/ppermute | solution.py:22
  304.4 14.9 %collective-permute-start.14 = (bf16[256,1024]{0,1:T(8,128)(2,1)S(1)}, bf16[256,1024]{0,1:T(8,128)(2,1)S(1)}, u32[]{:S(2)}, u32[]{:S(2)}) collective-permute-start(bf16[256,1024]{0,1:T(8,128)(2,1)S(1)} %slice.650), channel_id=1, source_target_pairs={{0,2},{1,3},{2,0},{3,1},{4,6},{5,7},{6,4},{7,5},{8,10},{9,11},{10,... | collective-permute-start | bytes 1572872 | tf_op jit(solution)/shard_map/ppermute | solution.py:22
  305.4 25.2 %collective-permute-start.21 = (bf16[256,1024]{0,1:T(8,128)(2,1)S(1)}, bf16[256,1024]{0,1:T(8,128)(2,1)S(1)}, u32[]{:S(2)}, u32[]{:S(2)}) collective-permute-start(bf16[256,1024]{0,1:T(8,128)(2,1)S(1)} %slice.648), channel_id=1, source_target_pairs={{0,2},{1,3},{2,0},{3,1},{4,6},{5,7},{6,4},{7,5},{8,10},{9,11},{10,... | collective-permute-start | bytes 1572872 | tf_op jit(solution)/shard_map/ppermute | solution.py:22
  307.5 34.3 %collective-permute-start.12 = (bf16[256,1024]{0,1:T(8,128)(2,1)S(1)}, bf16[256,1024]{0,1:T(8,128)(2,1)S(1)}, u32[]{:S(2)}, u32[]{:S(2)}) collective-permute-start(bf16[256,1024]{0,1:T(8,128)(2,1)S(1)} %slice.651), channel_id=1, source_target_pairs={{0,2},{1,3},{2,0},{3,1},{4,6},{5,7},{6,4},{7,5},{8,10},{9,11},{10,... | collective-permute-start | bytes 1572872 | tf_op jit(solution)/shard_map/ppermute | solution.py:22
  308.6 42.4 %copy-start.28 = (bf16[1024,1,1024]{0,2,1:T(8,128)(2,1)S(1)}, bf16[1024,1,1024]{0,2,1:T(8,128)(2,1)}, u32[]{:S(2)}) copy-start(bf16[1024,1,1024]{0,2,1:T(8,128)(2,1)} %copy.141) | copy-start | bytes 6291460
  308.6 42.4 %copy-start.104 = (f32[1024]{0:T(1024)S(1)}, f32[1024]{0:T(1024)}, u32[]{:S(2)}) copy-start(f32[1024]{0:T(1024)} %convert_element_type.491) | copy-start | bytes 12292
  308.6 42.3 %collective-permute-start.7 = (bf16[256,1024]{0,1:T(8,128)(2,1)S(1)}, bf16[256,1024]{0,1:T(8,128)(2,1)S(1)}, u32[]{:S(2)}, u32[]{:S(2)}) collective-permute-start(bf16[256,1024]{0,1:T(8,128)(2,1)S(1)} %slice.652), channel_id=1, source_target_pairs={{0,2},{1,3},{2,0},{3,1},{4,6},{5,7},{6,4},{7,5},{8,10},{9,11},{10,... | collective-permute-start | bytes 1572872 | tf_op jit(solution)/shard_map/ppermute | solution.py:22
  354.3 15.2 %collective-permute-start.22 = (bf16[256,1024]{0,1:T(8,128)(2,1)}, bf16[256,1024]{0,1:T(8,128)(2,1)}, u32[]{:S(2)}, u32[]{:S(2)}) collective-permute-start(bf16[256,1024]{0,1:T(8,128)(2,1)} %get-tuple-element.118), channel_id=1, source_target_pairs={{0,2},{1,3},{2,0},{3,1},{4,6},{5,7},{6,4},{7,5},{8,10},{9,11},{10,... | collective-permute-start | bytes 1572872 | tf_op jit(solution)/shard_map/ppermute | solution.py:22
  356.7 21.0 %collective-permute-start.15 = (bf16[256,1024]{0,1:T(8,128)(2,1)}, bf16[256,1024]{0,1:T(8,128)(2,1)}, u32[]{:S(2)}, u32[]{:S(2)}) collective-permute-start(bf16[256,1024]{0,1:T(8,128)(2,1)} %get-tuple-element.75), channel_id=1, source_target_pairs={{0,2},{1,3},{2,0},{3,1},{4,6},{5,7},{6,4},{7,5},{8,10},{9,11},{10,... | collective-permute-start | bytes 1572872 | tf_op jit(solution)/shard_map/ppermute | solution.py:22
  359.1 25.6 %collective-permute-start.23 = (bf16[256,1024]{0,1:T(8,128)(2,1)}, bf16[256,1024]{0,1:T(8,128)(2,1)}, u32[]{:S(2)}, u32[]{:S(2)}) collective-permute-start(bf16[256,1024]{0,1:T(8,128)(2,1)} %get-tuple-element.118), channel_id=1, source_target_pairs={{0,1},{1,0},{2,3},{3,2},{4,5},{5,4},{6,7},{7,6},{8,9},{9,8},{10,11... | collective-permute-start | bytes 1572872 | tf_op jit(solution)/shard_map/ppermute | solution.py:22
  359.1 22.4 %collective-permute-start.16 = (bf16[256,1024]{0,1:T(8,128)(2,1)}, bf16[256,1024]{0,1:T(8,128)(2,1)}, u32[]{:S(2)}, u32[]{:S(2)}) collective-permute-start(bf16[256,1024]{0,1:T(8,128)(2,1)} %get-tuple-element.75), channel_id=1, source_target_pairs={{0,1},{1,0},{2,3},{3,2},{4,5},{5,4},{6,7},{7,6},{8,9},{9,8},{10,11... | collective-permute-start | bytes 1572872 | tf_op jit(solution)/shard_map/ppermute | solution.py:22
  368.0 24.1 %copy-start.74 = (bf16[1024,64]{0,1:T(8,128)(2,1)S(1)}, bf16[1024,64]{0,1:T(8,128)(2,1)}, u32[]{:S(2)}) copy-start(bf16[1024,64]{0,1:T(8,128)(2,1)} %copy-done.73) | copy-start | bytes 393220
  368.0 24.1 %copy-start.76 = (bf16[1024,64]{0,1:T(8,128)(2,1)S(1)}, bf16[1024,64]{0,1:T(8,128)(2,1)}, u32[]{:S(2)}) copy-start(bf16[1024,64]{0,1:T(8,128)(2,1)} %copy-done.75) | copy-start | bytes 393220
  368.0 24.1 %copy-start.78 = (bf16[1024,64]{0,1:T(8,128)(2,1)S(1)}, bf16[1024,64]{0,1:T(8,128)(2,1)}, u32[]{:S(2)}) copy-start(bf16[1024,64]{0,1:T(8,128)(2,1)} %copy-done.77) | copy-start | bytes 393220
  368.0 24.1 %copy-start.80 = (bf16[1024,64]{0,1:T(8,128)(2,1)S(1)}, bf16[1024,64]{0,1:T(8,128)(2,1)}, u32[]{:S(2)}) copy-start(bf16[1024,64]{0,1:T(8,128)(2,1)} %copy-done.79) | copy-start | bytes 393220
  369.4 21.0 %collective-permute-start.24 = (bf16[256,1024]{0,1:T(8,128)(2,1)}, bf16[256,1024]{0,1:T(8,128)(2,1)S(1)}, u32[]{:S(2)}, u32[]{:S(2)}) collective-permute-start(bf16[256,1024]{0,1:T(8,128)(2,1)} %collective-permute-done.22), channel_id=1, source_target_pairs={{0,1},{1,0},{2,3},{3,2},{4,5},{5,4},{6,7},{7,6},{8,9},{9,8},{10,11... | collective-permute-start | bytes 1572872 | tf_op jit(solution)/shard_map/ppermute | solution.py:22
  377.7 69.2 %collective-permute-start.17 = (bf16[256,1024]{0,1:T(8,128)(2,1)}, bf16[256,1024]{0,1:T(8,128)(2,1)}, u32[]{:S(2)}, u32[]{:S(2)}) collective-permute-start(bf16[256,1024]{0,1:T(8,128)(2,1)} %collective-permute-done.15), channel_id=1, source_target_pairs={{0,1},{1,0},{2,3},{3,2},{4,5},{5,4},{6,7},{7,6},{8,9},{9,8},{10,11... | collective-permute-start | bytes 1572872 | tf_op jit(solution)/shard_map/ppermute | solution.py:22
  461.0 57.5 %collective-permute-start.37 = (bf16[512,256]{0,1:T(8,128)(2,1)}, bf16[512,256]{0,1:T(8,128)(2,1)}, u32[]{:S(2)}, u32[]{:S(2)}) collective-permute-start(bf16[512,256]{0,1:T(8,128)(2,1)} %dynamic-slice_convert_fusion.8), channel_id=1, source_target_pairs={{0,4},{4,0},{8,12},{12,8},{16,20},{20,16},{24,28},{28,24},{1,5},{5... | collective-permute-start | bytes 786440 | tf_op jit(solution)/shard_map/ppermute | solution.py:22
  507.4 22.4 %collective-permute-start.18 = (f32[512,1024]{0,1:T(8,128)S(1)}, f32[512,1024]{0,1:T(8,128)S(1)}, u32[]{:S(2)}, u32[]{:S(2)}) collective-permute-start(f32[512,1024]{0,1:T(8,128)S(1)} %pad_maximum_fusion.3), channel_id=1, source_target_pairs={{0,1},{1,0},{2,3},{3,2},{4,5},{5,4},{6,7},{7,6},{8,9},{9,8},{10,11... | collective-permute-start | bytes 6291464 | tf_op jit(solution)/shard_map/ppermute | solution.py:22
  510.2 25.3 %collective-permute-start.25 = (f32[512,1024]{0,1:T(8,128)S(1)}, f32[512,1024]{0,1:T(8,128)S(1)}, u32[]{:S(2)}, u32[]{:S(2)}) collective-permute-start(f32[512,1024]{0,1:T(8,128)S(1)} %pad_maximum_fusion.5), channel_id=1, source_target_pairs={{0,1},{1,0},{2,3},{3,2},{4,5},{5,4},{6,7},{7,6},{8,9},{9,8},{10,11... | collective-permute-start | bytes 6291464 | tf_op jit(solution)/shard_map/ppermute | solution.py:22
  515.8 45.0 %collective-permute-start.34 = (bf16[512,768]{1,0:T(8,128)(2,1)}, bf16[512,768]{1,0:T(8,128)(2,1)}, u32[]{:S(2)}, u32[]{:S(2)}) collective-permute-start(bf16[512,768]{1,0:T(8,128)(2,1)} %dynamic-slice_convert_fusion.2), channel_id=1, source_target_pairs={{0,4},{4,0},{8,12},{12,8},{16,20},{20,16},{24,28},{28,24},{1,5},{5... | collective-permute-start | bytes 2359304 | tf_op jit(solution)/shard_map/ppermute | solution.py:22
  519.6 9.6 %collective-permute-start.38 = (bf16[256,256]{0,1:T(8,128)(2,1)S(1)}, bf16[256,256]{0,1:T(8,128)(2,1)S(1)}, u32[]{:S(2)}, u32[]{:S(2)}) collective-permute-start(bf16[256,256]{0,1:T(8,128)(2,1)S(1)} %dynamic-slice_convert_fusion.10), channel_id=1, source_target_pairs={{0,8},{4,12},{8,0},{12,4},{16,24},{20,28},{24,16},{28,20},{1,9},{5... | collective-permute-start | bytes 393224 | tf_op jit(solution)/shard_map/ppermute | solution.py:22
  529.2 5.6 collective-permute-start.39
  530.3 14.9 %collective-permute-start.19 = (bf16[256,1024]{0,1:T(8,128)(2,1)S(1)}, bf16[256,1024]{0,1:T(8,128)(2,1)S(1)}, u32[]{:S(2)}, u32[]{:S(2)}) collective-permute-start(bf16[256,1024]{0,1:T(8,128)(2,1)S(1)} %slice.649), channel_id=1, source_target_pairs={{0,2},{1,3},{2,0},{3,1},{4,6},{5,7},{6,4},{7,5},{8,10},{9,11},{10,... | collective-permute-start | bytes 1572872 | tf_op jit(solution)/shard_map/ppermute | solution.py:22
  535.8 20.1 %copy-start.41 = (f32[256,1024]{0,1:T(8,128)S(1)}, f32[256,1024]{0,1:T(8,128)}, u32[]{:S(2)}) copy-start(f32[256,1024]{0,1:T(8,128)} %get-tuple-element.76) | copy-start | bytes 3145732
  535.9 19.0 %collective-permute-start.26 = (bf16[256,1024]{0,1:T(8,128)(2,1)S(1)}, bf16[256,1024]{0,1:T(8,128)(2,1)S(1)}, u32[]{:S(2)}, u32[]{:S(2)}) collective-permute-start(bf16[256,1024]{0,1:T(8,128)(2,1)S(1)} %slice.647), channel_id=1, source_target_pairs={{0,2},{1,3},{2,0},{3,1},{4,6},{5,7},{6,4},{7,5},{8,10},{9,11},{10,... | collective-permute-start | bytes 1572872 | tf_op jit(solution)/shard_map/ppermute | solution.py:22
  560.7 2.0 collective-permute-start.27
  562.8 4.2 collective-permute-start.28
  563.4 11.3 %collective-permute-start.35 = (bf16[256,768]{1,0:T(8,128)(2,1)S(1)}, bf16[256,768]{1,0:T(8,128)(2,1)S(1)}, u32[]{:S(2)}, u32[]{:S(2)}) collective-permute-start(bf16[256,768]{1,0:T(8,128)(2,1)S(1)} %dynamic-slice_convert_fusion.5), channel_id=1, source_target_pairs={{0,8},{4,12},{8,0},{12,4},{16,24},{20,28},{24,16},{28,20},{1,9},{5... | collective-permute-start | bytes 1179656 | tf_op jit(solution)/shard_map/ppermute | solution.py:22
  569.8 5.0 collective-permute-start.29
  574.8 4.0 collective-permute-start.30
  576.4 11.2 %collective-permute-start.36 = (bf16[128,768]{1,0:T(8,128)(2,1)S(1)}, bf16[128,768]{1,0:T(8,128)(2,1)S(1)}, u32[]{:S(2)}, u32[]{:S(2)}) collective-permute-start(bf16[128,768]{1,0:T(8,128)(2,1)S(1)} %dynamic-slice_convert_fusion.9), channel_id=1, source_target_pairs={{0,16},{4,20},{8,24},{12,28},{16,0},{20,4},{24,8},{28,12},{1,17},{... | collective-permute-start | bytes 589832 | tf_op jit(solution)/shard_map/ppermute | solution.py:22
  579.6 4.0 collective-permute-start.31
  583.8 6.0 collective-permute-start.32
  589.9 7.4 %collective-permute-start.33 = (f32[24064]{0:T(1024)S(1)}, f32[24064]{0:T(1024)S(1)}, u32[]{:S(2)}, u32[]{:S(2)}) collective-permute-start(f32[24064]{0:T(1024)S(1)} %pad_maximum_fusion.11), channel_id=1, source_target_pairs={{0,16},{4,20},{8,24},{12,28},{16,0},{20,4},{24,8},{28,12},{1,17},{... | collective-permute-start | bytes 288776 | tf_op jit(solution)/shard_map/ppermute | solution.py:22
  (126 other events, 687.1 us)

commit v2 on v1

v2 whole, which is shorter than its diff:
```python
import functools

import jax
import jax.numpy as jnp
from jax import lax
from jax.experimental import pallas as pl
from jax.experimental.pallas import tpu as pltpu
from jax.sharding import PartitionSpec as P

HEAD_DIM = 64
EPS = 1e-06
BF = jnp.bfloat16
F32 = jnp.float32
ROWS = ((0,), (0,))
COLS = ((1,), (1,))
MIB = 1 << 20
SCALE = HEAD_DIM**-0.5
SEND_FIRST = (3, 1, 2, 0)
NEAR_FIRST = (0, 2, 1, 3)


def dot(left, right, dims=((1,), (0,))):
    return lax.dot_general(left, right, (dims, ((), ())), preferred_element_type=F32)


def swap(value, axis, bit):
    pairs = [(i, i ^ bit) for i in range(lax.axis_size(axis))]
    return lax.ppermute(value, axis, pairs)


def normalize(values):
    centre = values - jnp.mean(values, axis=-1, keepdims=True)
    inverse = lax.rsqrt(jnp.mean(centre * centre, axis=-1, keepdims=True) + EPS)
    return centre * inverse, inverse


def norm_back(grad, normed, inverse):
    return inverse * (
        grad
        - jnp.mean(grad, axis=-1, keepdims=True)
        - normed * jnp.mean(grad * normed, axis=-1, keepdims=True)
    )


def gelu_pair(v):
    root = 0.7978845608028654
    square = v * v
    inner = jnp.tanh(v * (root + (root * 0.044715) * square))
    half = 0.5 + 0.5 * inner
    slope = half + (0.5 * v) * (1.0 - inner * inner) * (root + (3 * root * 0.044715) * square)
    return v * half, slope


def head_lanes(rows, cols, h):
    return lax.broadcasted_iota(jnp.int32, (rows, cols), 1) // HEAD_DIM == h


def spread(x, heads):
    rows, cols = x.shape
    zero = jnp.zeros_like(x)
    return jnp.concatenate([jnp.where(head_lanes(rows, cols, h), x, zero) for h in range(heads)], 0)


def gather_heads(x, heads):
    rows, cols = x.shape[0] // heads, x.shape[1]
    out = x[:rows]
    for h in range(1, heads):
        out = jnp.where(head_lanes(rows, cols, h), x[h * rows : (h + 1) * rows], out)
    return out


def whole(shape):
    return pl.BlockSpec(shape, lambda *_: (0,) * len(shape))


def shape_of(shape, dtype):
    return jax.ShapeDtypeStruct(shape, dtype)


def params(limit):
    return pltpu.CompilerParams(vmem_limit_bytes=limit * MIB)


def cost(flops, moved, special=0):
    return pl.CostEstimate(flops=int(flops), bytes_accessed=int(moved), transcendentals=int(special))


def project_kernel(tok_ref, mod_ref, w_ref, bias_ref, in_ref, q_ref, k_ref, v_ref):
    normed, _ = normalize(tok_ref[0].astype(F32))
    low = (normed * (1.0 + mod_ref[0, 1:2]) + mod_ref[0, 0:1]).astype(BF)
    in_ref[...] = low
    q_ref[...] = (dot(low, w_ref[0]) + bias_ref[0:1].astype(F32)).astype(BF)
    k_ref[...] = dot(low, w_ref[1]).astype(BF)
    v_ref[...] = (dot(low, w_ref[2]) + bias_ref[1:2].astype(F32)).astype(BF)


def project(tok, modulation, w3, bias, lat, block=512):
    _, seq, width = tok.shape
    cols = w3.shape[2]
    rows = lambda n: pl.BlockSpec((block, n), lambda i: (i, 0))
    return pl.pallas_call(
        project_kernel,
        out_shape=[shape_of((seq, width), BF)] + [shape_of((seq, cols), BF)] * 3,
        grid=(seq // block,),
        in_specs=[
            pl.BlockSpec((1, block, width), lambda i: (lat, i, 0)),
            pl.BlockSpec((1,) + modulation.shape[1:], lambda i: (lat, 0, 0)),
            whole(w3.shape),
            whole(bias.shape),
        ],
        out_specs=[rows(width), rows(cols), rows(cols), rows(cols)],
        compiler_params=params(40),
        cost_estimate=cost(6 * seq * width * cols, 4 * seq * width + 6 * seq * cols + 6 * width * cols),
        name="project",
    )(tok, modulation, w3, bias)


def attend_kernel(q_ref, k_ref, v_ref, mixed_ref, total_ref):
    rows, cols = q_ref.shape
    q, k, v = q_ref[...] * BF(SCALE), k_ref[...], v_ref[...]
    out = None
    for h in range(cols // HEAD_DIM):
        mine = head_lanes(rows, cols, h)
        scores = dot(jnp.where(mine, q, jnp.zeros_like(q)), k, COLS)
        largest = jnp.max(scores, axis=1, keepdims=True)
        powers = jnp.exp(scores - largest)
        total = jnp.sum(powers, axis=1, keepdims=True)
        part = dot((powers * (1.0 / total)).astype(BF), v)
        out = part if out is None else jnp.where(mine, part, out)
        log_total = jnp.broadcast_to(largest + jnp.log(total), (rows, 128))
        total_ref[0, :, h * rows : (h + 1) * rows] = log_total.T[:1]
    mixed_ref[...] = out.astype(BF)


def attend(q, k, v, block):
    seq, cols = q.shape
    heads = cols // HEAD_DIM
    rows = pl.BlockSpec((block, cols), lambda i: (i, 0))
    return pl.pallas_call(
        attend_kernel,
        out_shape=(
            shape_of((seq, cols), BF),
            shape_of((seq // block, 1, heads * block), F32),
        ),
        grid=(seq // block,),
        in_specs=[rows, whole((seq, cols)), whole((seq, cols))],
        out_specs=(rows, pl.BlockSpec((1, 1, heads * block), lambda i: (i, 0, 0))),
        compiler_params=params(40),
        cost_estimate=cost(16 * seq * seq * cols, 8 * seq * cols, seq * seq * heads),
        name="attend_forward",
    )(q, k, v)


def feed_kernel(
    order_ref, m0, m1, m2, m3, p0, p1, p2, p3, pb_ref, tok_ref, cot_ref, mod_ref, up_ref, ub_ref, down_ref,
    in_ref, hid_ref, pre_ref, gm_ref, upd_ref, send_u, keep_u, send_g, keep_g, gub_ref, gdb_ref,
):
    i = pl.program_id(0)
    row = lambda j: mod_ref[0, j : j + 1]
    update = pb_ref[...].astype(F32)
    for m, p in ((m0, p0), (m1, p1), (m2, p2), (m3, p3)):
        update = update + dot(m[...], p[...])
    upd_ref[...] = update
    normed, _ = normalize(tok_ref[0].astype(F32) + row(2) * update)
    low = (normed * (1.0 + row(4)) + row(3)).astype(BF)
    in_ref[...] = low
    act, slope = gelu_pair(dot(low, up_ref[...]) + ub_ref[...].astype(F32))
    hidden = act.astype(BF)
    hid_ref[...] = hidden
    grad_mlp = (row(5) * cot_ref[0].astype(F32)).astype(BF)
    gm_ref[...] = grad_mlp
    grad_pre = (dot(grad_mlp, down_ref[...], COLS) * slope).astype(BF)
    pre_ref[...] = grad_pre
    out_g = dot(grad_pre, up_ref[...], COLS)
    out_u = dot(hidden, down_ref[...])

    @pl.when(i < 2)
    def _():
        send_g[...] = out_g
        send_u[...] = out_u

    @pl.when(i >= 2)
    def _():
        keep_g[...] = out_g
        keep_u[...] = out_u

    @pl.when(i == 0)
    def _():
        gub_ref[...] = jnp.zeros_like(gub_ref)
        gdb_ref[...] = jnp.zeros_like(gdb_ref)

    gub_ref[...] += jnp.sum(grad_pre.astype(F32), axis=0, keepdims=True)
    gdb_ref[...] += jnp.sum(grad_mlp.astype(F32), axis=0, keepdims=True)


def feed(order, mixed, proj, proj_bias, tok, cot, modulation, up, up_bias, down, lat):
    _, seq, width = tok.shape
    block = seq // 4
    ff = up.shape[1]
    cols = mixed[0].shape[1]
    at = lambda n: pl.BlockSpec((block, n), lambda i, o: (o[i], 0))
    at3 = pl.BlockSpec((1, block, width), lambda i, o: (lat, o[i], 0))
    send = pl.BlockSpec((block, width), lambda i, o: (jnp.minimum(i, 1), 0))
    keep = pl.BlockSpec((block, width), lambda i, o: (jnp.maximum(i - 2, 0), 0))
    half = shape_of((2 * block, width), F32)
    flops = 2 * seq * width * (width + 4 * ff)
    return pl.pallas_call(
        feed_kernel,
        out_shape=[
            shape_of((seq, width), BF),
            shape_of((seq, ff), BF),
            shape_of((seq, ff), BF),
            shape_of((seq, width), BF),
            shape_of((block, width), F32),
            half,
            half,
            half,
            half,
            shape_of((1, ff), F32),
            shape_of((1, width), F32),
        ],
        grid_spec=pltpu.PrefetchScalarGridSpec(
            num_scalar_prefetch=1,
            grid=(4,),
            in_specs=[at(cols)] * 4
            + [whole((cols, width))] * 4
            + [whole((1, width)), at3, at3]
            + [pl.BlockSpec((1,) + modulation.shape[1:], lambda i, o: (lat, 0, 0))]
            + [whole(up.shape), whole((1, ff)), whole(down.shape)],
            out_specs=[at(width), at(ff), at(ff), at(width), whole((block, width))]
            + [send, keep, send, keep, whole((1, ff)), whole((1, width))],
        ),
        compiler_params=params(56),
        cost_estimate=cost(flops, 40 * MIB, seq * ff),
        name="feed",
    )(order, *mixed, *proj, proj_bias, tok, cot, modulation, up, up_bias, down)


def place_rows(pos_ref, send_ref, keep_ref, first, values, tiles):
    rows = send_ref.shape[0] * 2 // tiles
    for t in range(values.shape[0] // rows):
        pos = pos_ref[first + t]
        part = values[t * rows : (t + 1) * rows]

        @pl.when(pos < tiles // 2)
        def _():
            send_ref[pl.ds(pl.multiple_of(pos * rows, rows), rows), :] = part.astype(BF)

        @pl.when(pos >= tiles // 2)
        def _():
            keep_ref[pl.ds(pl.multiple_of((pos - tiles // 2) * rows, rows), rows), :] = part


def weight_kernel(tiles, terms, pos_ref, *refs):
    i = pl.program_id(0)
    block = refs[0].shape[1]
    rows = refs[-1].shape[0] * 2 // tiles
    for j in range(len(terms)):
        send_ref, keep_ref = refs[-2 * len(terms) + 2 * j], refs[-2 * len(terms) + 2 * j + 1]
        total = None
        for left, right in terms[j]:
            part = dot(refs[left][...], refs[right][...], ROWS)
            total = part if total is None else total + part
        place_rows(pos_ref.at[j], send_ref, keep_ref, i * (block // rows), total, tiles)


def weight_grads(pos, arrays, lefts, terms, widths, name, steps=4):
    tiles = pos.shape[1]
    seq, depth = arrays[lefts[0]].shape
    block = depth // steps
    specs = [
        pl.BlockSpec((seq, block), lambda i, o: (0, i)) if j in lefts else whole(a.shape)
        for j, a in enumerate(arrays)
    ]
    outs, out_specs = [], []
    for width in widths:
        outs += [shape_of((depth // 2, width), BF), shape_of((depth // 2, width), F32)]
        out_specs += [whole((depth // 2, width))] * 2
    flops = sum(2 * seq * depth * w * len(t) for w, t in zip(widths, terms))
    moved = sum(a.size * 2 for a in arrays) + sum(depth * w * 3 for w in widths)
    return pl.pallas_call(
        functools.partial(weight_kernel, tiles, terms),
        out_shape=outs,
        grid_spec=pltpu.PrefetchScalarGridSpec(
            num_scalar_prefetch=1, grid=(steps,), in_specs=specs, out_specs=out_specs
        ),
        compiler_params=params(56),
        cost_estimate=cost(flops, moved),
        name=name,
    )(pos, *arrays)


def proj_grad_kernel(tiles, quarter, order_ref, pos_ref, *refs):
    mixed, pieces, (send_ref, keep_ref) = refs[:2], refs[2:10], refs[10:]
    total = None
    for lat in range(2):
        for j in range(4):
            rows = pl.ds(pl.multiple_of(order_ref[j] * quarter, quarter), quarter)
            part = dot(mixed[lat][rows, :], pieces[4 * lat + j][...], ROWS)
            total = part if total is None else total + part
    place_rows(pos_ref, send_ref, keep_ref, 0, total.T, tiles)


def proj_grad(order, pos, mixed, pieces):
    tiles = pos.shape[0]
    quarter, width = pieces[0][0].shape
    cols = mixed[0].shape[1]
    args = list(mixed) + [p for four in pieces for p in four]
    return pl.pallas_call(
        functools.partial(proj_grad_kernel, tiles, quarter),
        out_shape=[shape_of((width // 2, cols), BF), shape_of((width // 2, cols), F32)],
        grid_spec=pltpu.PrefetchScalarGridSpec(
            num_scalar_prefetch=2,
            grid=(1,),
            in_specs=[whole(a.shape) for a in args],
            out_specs=[whole((width // 2, cols))] * 2,
        ),
        compiler_params=params(40),
        cost_estimate=cost(16 * quarter * width * cols, 8 * MIB),
        name="proj_grad",
    )(order, pos, *args)


def back_kernel(
    near_ref, order_ref, u0, u1, u2, u3, p_ref, q_ref, k_ref, v_ref, total_ref, w_ref, tok_ref,
    low_ref, send_ref, keep_ref, bias_ref, stat_ref, dk_acc, dv_acc,
):
    i = pl.program_id(0)
    rows, cols = q_ref.shape
    heads = cols // HEAD_DIM

    @pl.when(i == 0)
    def _():
        dk_acc[...] = jnp.zeros_like(dk_acc)
        dv_acc[...] = jnp.zeros_like(dv_acc)
        stat_ref[...] = jnp.zeros_like(stat_ref)

    @pl.when(i < 4)
    def _():
        update = u3[...]
        for j, piece in ((2, u2), (1, u1), (0, u0)):
            update = jnp.where(i == j, piece[...], update)
        grad = dot(update, p_ref[...], COLS).astype(BF)
        q = spread(q_ref[...] * BF(SCALE), heads)
        g = spread(grad, heads)
        k, v = k_ref[...], v_ref[...]
        probs = jnp.exp(dot(k, q, COLS) - total_ref[0])
        grad_probs = dot(v, g, COLS)
        inner = jnp.sum(probs * grad_probs, axis=0, keepdims=True)
        scores = (probs * (grad_probs - inner)).astype(BF)
        dv_acc[...] += dot(probs.astype(BF), g)
        dk_acc[...] += dot(scores, q)
        dq = gather_heads(dot(scores, k, ROWS), heads) * SCALE
        low_ref[0, pl.ds(pl.multiple_of(near_ref[i] * rows, rows), rows), :] = dq.astype(BF)

    @pl.when(i == 3)
    def _():
        low_ref[1] = dk_acc[...].astype(BF)
        low_ref[2] = dv_acc[...].astype(BF)
        for j in range(3):
            bias_ref[j : j + 1] = jnp.sum(low_ref[j].astype(F32), axis=0, keepdims=True)

    @pl.when(i >= 4)
    def _():
        here = pl.ds(pl.multiple_of(order_ref[jnp.maximum(i - 4, 0)] * rows, rows), rows)
        out = None
        for j in range(3):
            part = dot(low_ref[j, here, :], w_ref[j], COLS)
            out = part if out is None else out + part
        normed, _ = normalize(tok_ref[0].astype(F32))
        stat_ref[0:1] += jnp.sum(out, axis=0, keepdims=True)
        stat_ref[1:2] += jnp.sum(out * normed, axis=0, keepdims=True)

        @pl.when(i < 6)
        def _():
            send_ref[...] = out

        @pl.when(i >= 6)
        def _():
            keep_ref[...] = out


def attend_back(near, order, pieces, proj, q, k, v, total, w3, tok, lat):
    seq, cols = q.shape
    width = proj.shape[1]
    block = seq // 4
    heads = cols // HEAD_DIM
    first = lambda i, n, o: n[jnp.minimum(i, 3)]
    later = lambda i, n, o: o[jnp.maximum(i - 4, 0)]
    half = shape_of((2 * block, width), F32)
    flops = 20 * seq * seq * cols + 8 * seq * width * cols
    return pl.pallas_call(
        back_kernel,
        out_shape=[shape_of((3, seq, cols), BF), half, half, shape_of((8, cols), F32), shape_of((8, width), F32)],
        grid_spec=pltpu.PrefetchScalarGridSpec(
            num_scalar_prefetch=2,
            grid=(8,),
            in_specs=[whole((block, width))] * 4
            + [whole(proj.shape), pl.BlockSpec((block, cols), lambda *a: (first(*a), 0))]
            + [whole((seq, cols))] * 2
            + [pl.BlockSpec((1, 1, heads * block), lambda *a: (first(*a), 0, 0))]
            + [whole(w3.shape), pl.BlockSpec((1, block, width), lambda *a: (lat, later(*a), 0))],
            out_specs=[
                whole((3, seq, cols)),
                pl.BlockSpec((block, width), lambda i, n, o: (jnp.clip(i - 4, 0, 1), 0)),
                pl.BlockSpec((block, width), lambda i, n, o: (jnp.clip(i - 6, 0, 1), 0)),
                whole((8, cols)),
                whole((8, width)),
            ],
            scratch_shapes=[pltpu.VMEM((seq, cols), F32)] * 2,
        ),
        compiler_params=params(58),
        cost_estimate=cost(flops, 16 * MIB, seq * seq * heads),
        name="attend_backward",
    )(near, order, *pieces, proj, q, k, v, total, w3, tok)


def token_scatter(send, keep):
    rows = keep.shape[0] // 2
    kept = keep + swap(send, "tensor", 1)
    return kept[rows:] + swap(kept[:rows].astype(BF), "tensor", 2).astype(F32)


def pieces_of(own):
    far = swap(own, "tensor", 2)
    return own, far, swap(own, "tensor", 1), swap(far, "tensor", 1)


def dp_bits(size):
    return [1 << i for i in range(size.bit_length() - 1)]


def row_places(index, size, bits):
    away = jnp.arange(size, dtype=jnp.int32) ^ index
    place = jnp.zeros((size,), jnp.int32)
    for bit in bits:
        place = 2 * place + 1 - (away // bit) % 2
    return place


def dp_scatter(send, keep, bits):
    for bit in bits:
        kept = keep + swap(send, "dp", bit).astype(F32)
        half = kept.shape[0] // 2
        send, keep = kept[:half].astype(BF), kept[half:]
    return kept


def shards(
    tokens,
    condition,
    modulation_weight,
    modulation_bias,
    qkv_weight,
    qv_bias,
    proj_weight,
    proj_bias,
    up_weight,
    up_bias,
    down_weight,
    down_bias,
    cotangent,
):
    seq, lats, width = tokens.shape
    place = lax.axis_index("tensor")
    index = lax.axis_index("dp")
    size = lax.axis_size("dp")
    quarter = seq // 4
    mod_cols = modulation_weight.shape[1] // 4
    span = range(lats)
    order = jnp.array(SEND_FIRST, jnp.int32) ^ place
    near = jnp.array(NEAR_FIRST, jnp.int32) ^ place
    bits = dp_bits(size)
    other_bits = [bits[1], bits[0]] + bits[2:]
    places, other_places = row_places(index, size, bits), row_places(index, size, other_bits)
    proj = pieces_of(proj_weight)
    cond = condition.astype(F32)
    silu_low = jax.nn.silu(cond).astype(BF)
    modulation = (dot(silu_low, modulation_weight) + modulation_bias.astype(F32)).reshape(
        lats, 6, width
    )
    w3 = jnp.transpose(qkv_weight, (1, 0, 2))
    heads = w3.shape[2]
    tok = jnp.transpose(tokens, (1, 0, 2))
    cot = jnp.transpose(cotangent, (1, 0, 2))
    here = lambda value: lax.dynamic_slice_in_dim(value, place * quarter, quarter, 0)
    row = lambda l, i: modulation[l, i : i + 1]

    projected = [project(tok, modulation, w3, qv_bias, l) for l in span]
    mixed, log_total = zip(*[attend(*projected[l][1:], quarter) for l in span])
    mixed_all = [pieces_of(m) for m in mixed]

    fed = [
        feed(
            order, mixed_all[l], proj, proj_bias[None], tok, cot, modulation, up_weight,
            up_bias[None], down_weight, l,
        )
        for l in span
    ]
    mlp_in, hidden, grad_pre, grad_mlp, update = [[f[j] for f in fed] for j in range(5)]
    grad_mlp_in = [token_scatter(f[7], f[8]) for f in fed]
    mlp_sum = [token_scatter(f[5], f[6]) for f in fed]
    arrays = mlp_in + grad_pre + grad_mlp + hidden
    up_send, up_keep, down_send, down_keep = weight_grads(
        jnp.stack([places, other_places]),
        arrays,
        (0, 1, 4, 5),
        (((0, 2), (1, 3)), ((4, 6), (5, 7))),
        (hidden[0].shape[1],) * 2,
        "feed_grads",
    )
    up_shard = dp_scatter(up_send, up_keep, bits)
    down_shard = dp_scatter(down_send, down_keep, other_bits).T

    grad_stream, grad_update, stats, outs = [], [], [], []
    for l in span:
        stream = here(tok[l]).astype(F32) + row(l, 2) * update[l]
        normed, inverse = normalize(stream)
        cot_here = here(cot[l]).astype(F32)
        g = cot_here + norm_back(grad_mlp_in[l] * (1.0 + row(l, 4)), normed, inverse)
        grad_stream.append(g)
        grad_update.append(pieces_of((row(l, 2) * g).astype(BF)))
        mlp_update = mlp_sum[l] + down_bias.astype(F32)
        outs.append((stream + row(l, 5) * mlp_update).astype(BF))
        total = lambda v: jnp.sum(v, axis=0)
        stats.append(
            [
                total(g * update[l]),
                total(grad_mlp_in[l]),
                total(grad_mlp_in[l] * normed),
                total(cot_here * mlp_update),
            ]
        )

    proj_send, proj_keep = proj_grad(near, places, mixed, grad_update)
    proj_shard = dp_scatter(proj_send, proj_keep, bits).T
    backs = [
        attend_back(
            near, order, grad_update[l], proj_weight, *projected[l][1:], log_total[l], w3, tok, l
        )
        for l in span
    ]
    lows = [b[0] for b in backs]
    attend_in = [p[0] for p in projected]
    arrays = attend_in + [low[j] for low in lows for j in range(3)]
    sent = weight_grads(
        jnp.stack([other_places] * 3),
        arrays,
        (0, 1),
        tuple(((0, 2 + j), (1, 5 + j)) for j in range(3)),
        (heads,) * 3,
        "qkv_grads",
    )
    qkv_shard = dp_scatter(
        jnp.concatenate(sent[0::2], 1), jnp.concatenate(sent[1::2], 1), other_bits
    ).reshape(-1, 3, heads)

    grad_tokens, mod_part = [], []
    for l in span:
        grad_in = token_scatter(backs[l][1], backs[l][2])
        normed, inverse = normalize(here(tok[l]).astype(F32))
        grad_tokens.append(
            grad_stream[l] + norm_back(grad_in * (1.0 + row(l, 1)), normed, inverse)
        )
        mod_part.append(jnp.stack([backs[l][4][0], backs[l][4][1]] + stats[l]))

    mod = jnp.stack(mod_part).reshape(lats, -1)
    mod = mod + swap(mod, "tensor", 1)
    mod = mod + swap(mod, "tensor", 2)
    grad_modulation = mod.astype(BF)
    own_cols = lax.dynamic_slice_in_dim(grad_modulation, place * mod_cols, mod_cols, 1)
    own_weight = lax.dynamic_slice_in_dim(modulation_weight, place * mod_cols, mod_cols, 1)
    grad_silu = dot(own_cols, own_weight, COLS)
    grad_silu = grad_silu + swap(grad_silu, "tensor", 1)
    grad_silu = grad_silu + swap(grad_silu, "tensor", 2)
    grad_condition = jax.vjp(jax.nn.silu, cond)[1](grad_silu)[0]

    qkv_sum = backs[0][3] + backs[1][3]
    update_sum = sum(jnp.sum(p, axis=0, dtype=F32) for l in span for p in grad_update[l])
    biases = jnp.concatenate(
        [(fed[0][9] + fed[1][9])[0], (fed[0][10] + fed[1][10])[0], update_sum, qkv_sum[0], qkv_sum[2]]
    )
    gathered = jnp.concatenate([silu_low.astype(F32), own_cols.astype(F32)], 1)
    for bit in bits:
        other = swap(jnp.concatenate([gathered.reshape(-1), biases]), "dp", bit)
        theirs = other[: gathered.size].reshape(gathered.shape)
        biases = biases + other[gathered.size :]
        low = (index // bit) % 2 == 0
        gathered = jnp.concatenate(
            [jnp.where(low, gathered, theirs), jnp.where(low, theirs, gathered)], 0
        )
    all_silu = gathered[:, :width].astype(BF)
    all_cols = gathered[:, width:].astype(BF)
    mod_rows = width // size
    my_silu = lax.dynamic_slice_in_dim(all_silu, index * mod_rows, mod_rows, 1)
    mod_shard = dot(my_silu, all_cols, ROWS)
    mod_bias_sum = jnp.sum(all_cols, axis=0, dtype=F32)
    ff = up_weight.shape[1]
    ends = [ff, ff + width, ff + 2 * width, ff + 2 * width + heads]
    up_bias_sum, down_bias_sum, proj_bias_sum, q_sum, v_sum = jnp.split(biases, ends)
    return (
        jnp.stack(outs, 1),
        jnp.stack(grad_tokens, 1),
        grad_condition,
        mod_shard,
        mod_bias_sum,
        qkv_shard,
        jnp.stack([q_sum, v_sum]),
        proj_shard,
        proj_bias_sum,
        up_shard,
        up_bias_sum,
        down_shard,
        down_bias_sum,
    )


def solution(mesh):
    in_specs = (
        P(None, "dp", None),
        P("dp", None),
        P(),
        P(),
        P(None, None, "tensor"),
        P(None, "tensor"),
        P("tensor", None),
        P(),
        P(None, "tensor"),
        P("tensor"),
        P("tensor", None),
        P(),
        P(None, "dp", None),
    )
    out_specs = (
        P("tensor", "dp", None),
        P("tensor", "dp", None),
        P("dp", None),
        P("dp", "tensor"),
        P("tensor"),
        P("dp", None, "tensor"),
        P(None, "tensor"),
        P("tensor", "dp"),
        P(),
        P("dp", "tensor"),
        P("tensor"),
        P("tensor", "dp"),
        P(),
    )
    return jax.shard_map(shards, mesh=mesh, in_specs=in_specs, out_specs=out_specs, check_vma=False)
```

time: 608 us -> 400 us (0.66)
  matrix products: 182 us -> 10.4 us
  Pallas kernels: 0 us -> 151 us
  local copies, waits for them, and re-layouts: 132 us -> 42.6 us
  other arithmetic: 107 us -> 48.8 us
  waiting for transfers between devices: 134 us -> 99 us
    dot_general x81 -> x3, matrix products: 182 us -> 10.4 us  [dot(): lax.dot_general(left, right, (dims, ((), ())), preferred_element_type=F32)]
    pallas_call x0 -> x11, Pallas kernels: none -> 151 us  [the longest x2 48.9 us: attend_back(): pl.pallas_call(back_kernel, out_shape=[shape_of((3, seq, cols), BF), half...]
    unnamed x301 -> x178, local copies, waits for them, and re-layouts: 66.2 us -> 25.8 us
    ppermute x46, waiting for transfers between devices: 134 us -> 99 us  [swap(): return lax.ppermute(value, axis, pairs)]
    convert_element_type x13 -> x0, other arithmetic: 23.9 us -> none  [the longest x8 18.1 us: attend_back(): grad_scores = (probs * (grad_probs - inner)).astype(BF)]
    reduce_sum x21 -> x8, other arithmetic: 21.9 us -> 6.87 us  [the longest x7 4.88 us: shards(): jnp.sum(p, axis=0, dtype=F32)]
    dynamic_update_slice x8 -> x0, local copies, waits for them, and re-layouts: 13.6 us -> none  [shards(): lax.dynamic_update_slice_in_dim(whole, piece, (place ^ k) * quarter, 0)]
    slice x3 -> x13, local copies, waits for them, and re-layouts: 20.4 us -> 10.4 us  [the longest x1 4.71 us: shards(): cot_here = here(cot[l]).astype(F32)]
  transfers between devices with their start and end apart: 46 -> 46, of which waited for: 18 -> 14; matrix products, arithmetic and copies ran while one was open for 47% -> 20% of each run, Pallas kernels for 0% -> 35%
where the time goes in v2:
time: 400 us; the launch traced here: 396 us
  Pallas kernels  151 us (38%)
  waiting for transfers between devices  99 us (25%)
  other arithmetic  48.8 us (12%)
  local copies, waits for them, and re-layouts  42.6 us (11%)
  starting transfers between devices  42.2 us (11%)
  matrix products  10.4 us (3%)
    ppermute x46, waiting for transfers between devices, swap(): return lax.ppermute(value, axis, pairs)  99 us
    pallas_call x2, Pallas kernels, attend_back(): pl.pallas_call(back_kernel, out_shape=[shape_of((3, seq, cols), BF), half...  48.9 us
    pallas_call x2, Pallas kernels, feed(): pl.pallas_call(feed_kernel, out_shape=[shape_of((seq, width), BF), shape_...  45.9 us
    ppermute x46, starting transfers between devices, swap(): return lax.ppermute(value, axis, pairs)  42.2 us
    pallas_call x2, Pallas kernels, weight_grads(): pl.pallas_call(functools.partial(weight_kernel, tiles, terms), out_shape=...  31.8 us
    unnamed x178, local copies, waits for them, and re-layouts  25.8 us
    pallas_call x2, Pallas kernels, attend(): pl.pallas_call(attend_kernel, out_shape=(shape_of((seq, cols), BF), shape...  15.5 us
    add x6, other arithmetic, token_scatter(): kept = keep + swap(send, 'tensor', 1)  12.8 us
  transfers between devices with their start and end apart: 46, of which 14 were waited for; matrix products, arithmetic and copies ran while one was open for 20% of the time, Pallas kernels for 35%

profile of v2, /device:TPU:0, one launch (start us, length us, event | category | flops | bytes accessed | tf_op | source)
XLA Modules:
  0.0 396.0 jit_solution(6719325875742211286)
XLA Ops:
  0.7 5.5 %copy.48 = bf16[1024,2,1024]{2,0,1:T(8,128)(2,1)} copy(bf16[1024,2,1024]{2,1,0:T(2,128)(2,1)} %param.15) | data formatting | bytes 8388608 | tf_op args[0]
  6.2 6.4 %convolution_add_fusion = f32[2,6144]{1,0:T(2,128)S(1)} fusion(bf16[1024,6144]{1,0:T(8,128)(2,1)} %param.17, f32[6144]{0:T(1024)S(1)} %convert_element_type.157, bf16[2,1024]{1,0:T(2,128)(2,1)S(1)} %copy-done.59), kind=kOutput, calls=%fused_computation | convolution fusion | flops 25190400 | bytes 12660736 | tf_op jit(solution)/shard_map/dot_general | solution.py:23
  12.7 2.2 copy-done
  14.9 3.2 project.2
  18.2 7.8 %attend_forward.2 = (bf16[1024,256]{1,0:T(8,128)(2,1)S(1)}, f32[4,1,1024]{2,1,0:T(1,128)S(1)}) custom-call(bf16[1024,256]{1,0:T(8,128)(2,1)S(1)} %get-tuple-element.69.q_ref, bf16[1024,256]{1,0:T(8,128)(2,1)S(1)} %get-tuple-element.70.k_ref, bf16[1024,256]{1,0:T(8,128)(2,1)S(1)} %get-tuple-element.71.v_ref), custom_call_target="tpu_custom_call" | custom-call | flops 4294967296 | bytes 2097152 | tf_op jit(solution)/shard_map/attend_forward/pallas_call | solution.py:139
  26.0 3.0 collective-permute-start
  29.6 3.0 project.3
  32.7 7.8 %attend_forward.3 = (bf16[1024,256]{1,0:T(8,128)(2,1)S(1)}, f32[4,1,1024]{2,1,0:T(1,128)S(1)}) custom-call(bf16[1024,256]{1,0:T(8,128)(2,1)S(1)} %get-tuple-element.76.q_ref, bf16[1024,256]{1,0:T(8,128)(2,1)S(1)} %get-tuple-element.77.k_ref, bf16[1024,256]{1,0:T(8,128)(2,1)S(1)} %get-tuple-element.78.v_ref), custom_call_target="tpu_custom_call" | custom-call | flops 4294967296 | bytes 2097152 | tf_op jit(solution)/shard_map/attend_forward/pallas_call | solution.py:139
  41.1 1.7 collective-permute-start.8
  42.8 1.9 fusion.71
  47.5 5.7 %collective-permute-done.3.p1 = bf16[256,1024]{1,0:T(8,128)(2,1)} collective-permute-done((bf16[256,1024]{1,0:T(8,128)(2,1)}, bf16[256,1024]{1,0:T(8,128)(2,1)}, u32[]{:S(2)}, u32[]{:S(2)}) %collective-permute-start.3) | collective-permute-done | bytes 524320 | tf_op jit(solution)/shard_map/ppermute | solution.py:28
  53.8 5.5 %copy.47 = bf16[1024,2,1024]{2,0,1:T(8,128)(2,1)} copy(bf16[1024,2,1024]{2,1,0:T(2,128)(2,1)} %param.27) | data formatting | bytes 8388608 | tf_op args[12]
  60.5 4.7 %fusion.70 = (bf16[1,1024,1024]{2,1,0:T(8,128)(2,1)}, bf16[1,1024,1024]{2,1,0:T(8,128)(2,1)}) fusion(bf16[2,1024,1024]{2,1,0:T(8,128)(2,1)} %bitcast.138), kind=kLoop, calls=%fused_computation.235 | loop fusion | bytes 8388608 | tf_op jit(solution)/shard_map/slice | solution.py:519
  65.8 23.1 %feed.2 = (bf16[1024,1024]{1,0:T(8,128)(2,1)}, bf16[1024,1024]{1,0:T(8,128)(2,1)}, bf16[1024,1024]{1,0:T(8,128)(2,1)}, bf16[1024,1024]{1,0:T(8,128)(2,1)}, f32[2...) custom-call(s32[4]{0:T(128)} %broadcast_xor_fusion.1.order_ref, ...), custom_call_target="tpu_custom_call" | custom-call | flops 10737418240 | bytes 41943040 | tf_op jit(solution)/shard_map/feed/pallas_call | solution.py:207
  91.0 22.8 %feed.3 = (bf16[1024,1024]{1,0:T(8,128)(2,1)}, bf16[1024,1024]{1,0:T(8,128)(2,1)}, bf16[1024,1024]{1,0:T(8,128)(2,1)}, bf16[1024,1024]{1,0:T(8,128)(2,1)}, f32[2...) custom-call(s32[4]{0:T(128)} %broadcast_xor_fusion.1.order_ref, ...), custom_call_target="tpu_custom_call" | custom-call | flops 10737418240 | bytes 41943040 | tf_op jit(solution)/shard_map/feed/pallas_call | solution.py:207
  114.5 1.7 fusion.68
  116.5 19.2 %feed_grads.1 = (bf16[512,1024]{1,0:T(8,128)(2,1)}, f32[512,1024]{1,0:T(8,128)}, bf16[512,1024]{1,0:T(8,128)(2,1)}, f32[512,1024]{1,0:T(8,128)}) custom-call(s32[2,8]{1,0:T(2,128)} %pad_add_fusion.pos_ref, bf16[1024,1024]{1,0:T(8,128)(2,1)} %get-tuple-element.113.refs_0_, bf16[1024,1024]{1,0:T(8,128)(2,1)} %get-tuple-element.114.refs_1_, ...), custom_call_target="tpu_custom_call" | custom-call | flops 8589934592 | bytes 23068672 | tf_op jit(solution)/shard_map/feed_grads/pallas_call | solution.py:281
  135.7 2.1 collective-permute-start.40
  138.2 1.6 collective-permute-start.43
  141.4 2.1 add.437
  143.6 18.2 %collective-permute-done.40 = bf16[512,1024]{1,0:T(8,128)(2,1)S(1)} collective-permute-done((bf16[512,1024]{1,0:T(8,128)(2,1)}, bf16[512,1024]{1,0:T(8,128)(2,1)S(1)}, u32[]{:S(2)}, u32[]{:S(2)}) %collective-permute-start.40) | collective-permute-done | bytes 1048608 | tf_op jit(solution)/shard_map/ppermute | solution.py:28
  161.8 1.8 collective-permute-start.14
  164.0 1.6 collective-permute-start.41
  166.2 1.5 collective-permute-start.44
  167.7 2.1 add.426
  170.7 2.2 add.432
  173.0 1.4 collective-permute-start.12
  174.4 2.0 add.449
  176.6 1.8 collective-permute-start.21
  179.0 8.8 %collective-permute-done.7 = bf16[256,1024]{1,0:T(8,128)(2,1)S(1)} collective-permute-done((bf16[256,1024]{1,0:T(8,128)(2,1)S(1)}, bf16[256,1024]{1,0:T(8,128)(2,1)S(1)}, u32[]{:S(2)}, u32[]{:S(2)}) %collective-permute-start.7) | collective-permute-done | bytes 524320 | tf_op jit(solution)/shard_map/ppermute | solution.py:28
  187.8 2.5 convert_reduce_fusion.9
  190.3 1.8 collective-permute-start.15
  192.2 18.1 %collective-permute-done.21 = bf16[256,1024]{1,0:T(8,128)(2,1)S(1)} collective-permute-done((bf16[256,1024]{1,0:T(8,128)(2,1)S(1)}, bf16[256,1024]{1,0:T(8,128)(2,1)S(1)}, u32[]{:S(2)}, u32[]{:S(2)}) %collective-permute-start.21) | collective-permute-done | bytes 524320 | tf_op jit(solution)/shard_map/ppermute | solution.py:28
  210.9 3.0 fusion.26
  213.9 1.8 collective-permute-start.22
  215.7 5.8 %collective-permute-done.15.u1.refs_3_ = bf16[256,1024]{1,0:T(8,128)(2,1)S(1)} collective-permute-done((bf16[256,1024]{1,0:T(8,128)(2,1)S(1)}, bf16[256,1024]{1,0:T(8,128)(2,1)S(1)}, u32[]{:S(2)}, u32[]{:S(2)}) %collective-permute-start.15) | collective-permute-done | bytes 524320 | tf_op jit(solution)/shard_map/ppermute | solution.py:28
  222.4 2.9 collective-permute-start.42
  226.5 5.1 %collective-permute-done.22.u1.refs_7_ = bf16[256,1024]{1,0:T(8,128)(2,1)S(1)} collective-permute-done((bf16[256,1024]{1,0:T(8,128)(2,1)S(1)}, bf16[256,1024]{1,0:T(8,128)(2,1)S(1)}, u32[]{:S(2)}, u32[]{:S(2)}) %collective-permute-start.22) | collective-permute-done | bytes 524320 | tf_op jit(solution)/shard_map/ppermute | solution.py:28
  232.5 24.5 %attend_backward.2 = (bf16[3,1024,256]{2,1,0:T(8,128)(2,1)}, f32[512,1024]{1,0:T(8,128)}, f32[512,1024]{1,0:T(8,128)}, f32[8,256]{1,0:T(8,128)}, f32[8,1024]{1,0:T(8,128)}) custom-call(s32[4]{0:T(128)} %broadcast_xor_fusion.near_ref.order_ref, s32[4]{0:T(128)} %broadcast_xor_fusion.1.order_ref, bf16[256,1024]{1,0:T(8,128)(2,1)} %copy-done.16, ...), custom_call_target="tpu_custom_call" | custom-call | flops 7516192768 | bytes 16777216 | tf_op jit(solution)/shard_map/attend_backward/pallas_call | solution.py:392
  258.5 24.4 %attend_backward.3 = (bf16[3,1024,256]{2,1,0:T(8,128)(2,1)}, f32[512,1024]{1,0:T(8,128)}, f32[512,1024]{1,0:T(8,128)}, f32[8,256]{1,0:T(8,128)}, f32[8,1024]{1,0:T(8,128)}) custom-call(s32[4]{0:T(128)} %broadcast_xor_fusion.near_ref.order_ref, s32[4]{0:T(128)} %broadcast_xor_fusion.1.order_ref, bf16[256,1024]{1,0:T(8,128)(2,1)} %copy-done.2, ...), custom_call_target="tpu_custom_call" | custom-call | flops 7516192768 | bytes 16777216 | tf_op jit(solution)/shard_map/attend_backward/pallas_call | solution.py:392
  287.2 2.0 copy.38
  294.7 12.7 %qkv_grads.1 = (bf16[512,256]{1,0:T(8,128)(2,1)}, f32[512,256]{1,0:T(8,128)}, bf16[512,256]{1,0:T(8,128)(2,1)}, f32[512,256]{1,0:T(8,128)}, bf16[512,256]{1,0:T(8,128)(2,1)}, /*index=5*/f32[512,256]{1,0:T(8,128)}) custom-call(s32[3,8]{1,0:T(4,128)} %stack.98.pos_ref, bf16[1024,1024]{1,0:T(8,128)(2,1)} %copy-done.26, bf16[1024,1024]{1,0:T(8,128)(2,1)} %copy-done.27, ...), custom_call_target="tpu_custom_call" | custom-call | flops 3221225472 | bytes 9699328 | tf_op jit(solution)/shard_map/qkv_grads/pallas_call | solution.py:281
  307.4 2.0 pad_maximum_fusion.2
  309.4 1.7 collective-permute-start.34
  311.1 2.1 add.443
  313.3 1.6 collective-permute-start.19
  315.0 2.3 add.455
  318.0 2.2 proj_grad.1
  320.2 1.5 collective-permute-start.37
  323.6 4.5 %collective-permute-done.19 = bf16[256,1024]{1,0:T(8,128)(2,1)S(1)} collective-permute-done((bf16[256,1024]{1,0:T(8,128)(2,1)S(1)}, bf16[256,1024]{1,0:T(8,128)(2,1)S(1)}, u32[]{:S(2)}, u32[]{:S(2)}) %collective-permute-start.19) | collective-permute-done | bytes 524320 | tf_op jit(solution)/shard_map/ppermute | solution.py:28
  328.1 10.5 %collective-permute-done.26 = bf16[256,1024]{1,0:T(8,128)(2,1)S(1)} collective-permute-done((bf16[256,1024]{1,0:T(8,128)(2,1)S(1)}, bf16[256,1024]{1,0:T(8,128)(2,1)S(1)}, u32[]{:S(2)}, u32[]{:S(2)}) %collective-permute-start.26) | collective-permute-done | bytes 524320 | tf_op jit(solution)/shard_map/ppermute | solution.py:28
  338.6 2.0 fusion.35
  340.7 1.5 multiply_reduce_fusion.1
  342.2 3.3 multiply_reduce_fusion.3
  347.2 1.7 collective-permute-start.28
  348.9 3.8 collective-permute-done.38
  352.8 2.6 collective-permute-start.39
  355.4 2.8 fusion
  359.4 1.7 collective-permute-start.30
  362.6 1.5 collective-permute-start.35
  365.6 8.2 %collective-permute-done.35 = bf16[256,768]{1,0:T(8,128)(2,1)S(1)} collective-permute-done((bf16[256,768]{1,0:T(8,128)(2,1)S(1)}, bf16[256,768]{1,0:T(8,128)(2,1)S(1)}, u32[]{:S(2)}, u32[]{:S(2)}) %collective-permute-start.35) | collective-permute-done | bytes 393248 | tf_op jit(solution)/shard_map/ppermute | solution.py:28
  376.9 7.4 %collective-permute-done.36 = bf16[128,768]{1,0:T(8,128)(2,1)S(1)} collective-permute-done((bf16[128,768]{1,0:T(8,128)(2,1)S(1)}, bf16[128,768]{1,0:T(8,128)(2,1)S(1)}, u32[]{:S(2)}, u32[]{:S(2)}) %collective-permute-start.36) | collective-permute-done | bytes 196640 | tf_op jit(solution)/shard_map/ppermute | solution.py:28
  387.4 2.9 copy.39
  390.4 2.3 collective-permute-done.33
  (347 shorter events, 46.3 us)
Async XLA Ops:
  12.7 34.6 %copy-start.22 = (f32[2,6,1024]{2,1,0:T(8,128)}, f32[2,6,1024]{2,1,0:T(8,128)S(1)}, u32[]{:S(2)}) copy-start(f32[2,6,1024]{2,1,0:T(8,128)S(1)} %reshape.398.mod_ref) | copy-start | bytes 147460
  18.2 11.4 %copy-start.1 = (bf16[1024,2,1024]{2,0,1:T(8,128)(2,1)S(1)}, bf16[1024,2,1024]{2,0,1:T(8,128)(2,1)}, u32[]{:S(2)}) copy-start(bf16[1024,2,1024]{2,0,1:T(8,128)(2,1)} %copy.48) | copy-start | bytes 12582916
  26.0 21.4 %collective-permute-start = (bf16[1024,256]{1,0:T(8,128)(2,1)S(1)}, bf16[1024,256]{1,0:T(8,128)(2,1)}, u32[]{:S(2)}, u32[]{:S(2)}) collective-permute-start(bf16[1024,256]{1,0:T(8,128)(2,1)S(1)} %get-tuple-element.72.m0.refs_0_), channel_id=1, source_target_pairs={{0,2},{1,3},{2,0},{3,1},{4,6},{5,7},{6,4},{7,5},{8,10},{9,11},{10,... | collective-permute-start | bytes 1572872 | tf_op jit(solution)/shard_map/ppermute | solution.py:28
  29.0 36.2 %collective-permute-start.1 = (bf16[1024,256]{1,0:T(8,128)(2,1)S(1)}, bf16[1024,256]{1,0:T(8,128)(2,1)}, u32[]{:S(2)}, u32[]{:S(2)}) collective-permute-start(bf16[1024,256]{1,0:T(8,128)(2,1)S(1)} %get-tuple-element.72.m0.refs_0_), channel_id=1, source_target_pairs={{0,1},{1,0},{2,3},{3,2},{4,5},{5,4},{6,7},{7,6},{8,9},{9,8},{10,11... | collective-permute-start | bytes 1572872 | tf_op jit(solution)/shard_map/ppermute | solution.py:28
  29.0 24.1 %collective-permute-start.3 = (bf16[256,1024]{1,0:T(8,128)(2,1)}, bf16[256,1024]{1,0:T(8,128)(2,1)}, u32[]{:S(2)}, u32[]{:S(2)}) collective-permute-start(bf16[256,1024]{1,0:T(8,128)(2,1)} %p_ref.3), channel_id=1, source_target_pairs={{0,2},{1,3},{2,0},{3,1},{4,6},{5,7},{6,4},{7,5},{8,10},{9,11},{10,... | collective-permute-start | bytes 1572872 | tf_op jit(solution)/shard_map/ppermute | solution.py:28
  29.2 36.6 %collective-permute-start.4 = (bf16[256,1024]{1,0:T(8,128)(2,1)}, bf16[256,1024]{1,0:T(8,128)(2,1)}, u32[]{:S(2)}, u32[]{:S(2)}) collective-permute-start(bf16[256,1024]{1,0:T(8,128)(2,1)} %p_ref.3), channel_id=1, source_target_pairs={{0,1},{1,0},{2,3},{3,2},{4,5},{5,4},{6,7},{7,6},{8,9},{9,8},{10,11... | collective-permute-start | bytes 1572872 | tf_op jit(solution)/shard_map/ppermute | solution.py:28
  41.1 24.2 %copy-start.20 = (bf16[1024,256]{1,0:T(8,128)(2,1)}, bf16[1024,256]{1,0:T(8,128)(2,1)S(1)}, u32[]{:S(2)}) copy-start(bf16[1024,256]{1,0:T(8,128)(2,1)S(1)} %get-tuple-element.79.m0.refs_1_) | copy-start | bytes 1572868
  41.1 24.7 %collective-permute-start.8 = (bf16[1024,256]{1,0:T(8,128)(2,1)S(1)}, bf16[1024,256]{1,0:T(8,128)(2,1)}, u32[]{:S(2)}, u32[]{:S(2)}) collective-permute-start(bf16[1024,256]{1,0:T(8,128)(2,1)S(1)} %get-tuple-element.79.m0.refs_1_), channel_id=1, source_target_pairs={{0,2},{1,3},{2,0},{3,1},{4,6},{5,7},{6,4},{7,5},{8,10},{9,11},{10,... | collective-permute-start | bytes 1572872 | tf_op jit(solution)/shard_map/ppermute | solution.py:28
  42.8 10.4 %copy-start.75 = (bf16[1024]{0:T(1024)(128)(2,1)S(1)}, bf16[1024]{0:T(1024)(128)(2,1)}, u32[]{:S(2)}) copy-start(bf16[1024]{0:T(1024)(128)(2,1)} %param.22) | copy-start | bytes 6148
  44.7 93.1 %copy-start.36 = (bf16[1,1024,1024]{2,1,0:T(8,128)(2,1)}, bf16[1,1024,1024]{2,1,0:T(8,128)(2,1)S(1)}, u32[]{:S(2)}) copy-start(bf16[1,1024,1024]{2,1,0:T(8,128)(2,1)S(1)} %get-tuple-element.181) | copy-start | bytes 6291460
  47.4 18.5 %collective-permute-start.2 = (bf16[1024,256]{1,0:T(8,128)(2,1)}, bf16[1024,256]{1,0:T(8,128)(2,1)}, u32[]{:S(2)}, u32[]{:S(2)}) collective-permute-start(bf16[1024,256]{1,0:T(8,128)(2,1)} %collective-permute-done.m1), channel_id=1, source_target_pairs={{0,1},{1,0},{2,3},{3,2},{4,5},{5,4},{6,7},{7,6},{8,9},{9,8},{10,11... | collective-permute-start | bytes 1572872 | tf_op jit(solution)/shard_map/ppermute | solution.py:28
  53.1 12.7 %collective-permute-start.5 = (bf16[256,1024]{1,0:T(8,128)(2,1)}, bf16[256,1024]{1,0:T(8,128)(2,1)}, u32[]{:S(2)}, u32[]{:S(2)}) collective-permute-start(bf16[256,1024]{1,0:T(8,128)(2,1)} %collective-permute-done.3.p1), channel_id=1, source_target_pairs={{0,1},{1,0},{2,3},{3,2},{4,5},{5,4},{6,7},{7,6},{8,9},{9,8},{10,11... | collective-permute-start | bytes 1572872 | tf_op jit(solution)/shard_map/ppermute | solution.py:28
  65.2 24.2 %collective-permute-start.9 = (bf16[1024,256]{1,0:T(8,128)(2,1)S(1)}, bf16[1024,256]{1,0:T(8,128)(2,1)S(1)}, u32[]{:S(2)}, u32[]{:S(2)}) collective-permute-start(bf16[1024,256]{1,0:T(8,128)(2,1)S(1)} %get-tuple-element.79.m0.refs_1_), channel_id=1, source_target_pairs={{0,1},{1,0},{2,3},{3,2},{4,5},{5,4},{6,7},{7,6},{8,9},{9,8},{10,11... | collective-permute-start | bytes 1572872 | tf_op jit(solution)/shard_map/ppermute | solution.py:28
  65.8 23.7 %collective-permute-start.10 = (bf16[1024,256]{1,0:T(8,128)(2,1)}, bf16[1024,256]{1,0:T(8,128)(2,1)S(1)}, u32[]{:S(2)}, u32[]{:S(2)}) collective-permute-start(bf16[1024,256]{1,0:T(8,128)(2,1)} %collective-permute-done.8.m1), channel_id=1, source_target_pairs={{0,1},{1,0},{2,3},{3,2},{4,5},{5,4},{6,7},{7,6},{8,9},{9,8},{10,11... | collective-permute-start | bytes 1572872 | tf_op jit(solution)/shard_map/ppermute | solution.py:28
  88.9 77.3 %collective-permute-start.6 = (f32[512,1024]{1,0:T(8,128)}, f32[512,1024]{1,0:T(8,128)}, u32[]{:S(2)}, u32[]{:S(2)}) collective-permute-start(f32[512,1024]{1,0:T(8,128)} %get-tuple-element.75), channel_id=1, source_target_pairs={{0,1},{1,0},{2,3},{3,2},{4,5},{5,4},{6,7},{7,6},{8,9},{9,8},{10,11... | collective-permute-start | bytes 6291464 | tf_op jit(solution)/shard_map/ppermute | solution.py:28
  113.8 56.2 %collective-permute-start.11 = (f32[512,1024]{1,0:T(8,128)}, f32[512,1024]{1,0:T(8,128)}, u32[]{:S(2)}, u32[]{:S(2)}) collective-permute-start(f32[512,1024]{1,0:T(8,128)} %get-tuple-element.82), channel_id=1, source_target_pairs={{0,1},{1,0},{2,3},{3,2},{4,5},{5,4},{6,7},{7,6},{8,9},{9,8},{10,11... | collective-permute-start | bytes 6291464 | tf_op jit(solution)/shard_map/ppermute | solution.py:28
  113.9 59.0 %collective-permute-start.20 = (f32[512,1024]{1,0:T(8,128)}, f32[512,1024]{1,0:T(8,128)}, u32[]{:S(2)}, u32[]{:S(2)}) collective-permute-start(f32[512,1024]{1,0:T(8,128)} %get-tuple-element.89), channel_id=1, source_target_pairs={{0,1},{1,0},{2,3},{3,2},{4,5},{5,4},{6,7},{7,6},{8,9},{9,8},{10,11... | collective-permute-start | bytes 6291464 | tf_op jit(solution)/shard_map/ppermute | solution.py:28
  114.4 23.9 %collective-permute-start.13 = (f32[512,1024]{1,0:T(8,128)}, f32[512,1024]{1,0:T(8,128)}, u32[]{:S(2)}, u32[]{:S(2)}) collective-permute-start(f32[512,1024]{1,0:T(8,128)} %get-tuple-element.84), channel_id=1, source_target_pairs={{0,1},{1,0},{2,3},{3,2},{4,5},{5,4},{6,7},{7,6},{8,9},{9,8},{10,11... | collective-permute-start | bytes 6291464 | tf_op jit(solution)/shard_map/ppermute | solution.py:28
  116.5 21.4 %copy-start.40 = (f32[256,1024]{1,0:T(8,128)S(1)}, f32[256,1024]{1,0:T(8,128)}, u32[]{:S(2)}) copy-start(f32[256,1024]{1,0:T(8,128)} %get-tuple-element.73) | copy-start | bytes 3145732
  135.7 26.0 %collective-permute-start.40 = (bf16[512,1024]{1,0:T(8,128)(2,1)}, bf16[512,1024]{1,0:T(8,128)(2,1)S(1)}, u32[]{:S(2)}, u32[]{:S(2)}) collective-permute-start(bf16[512,1024]{1,0:T(8,128)(2,1)} %get-tuple-element.122), channel_id=1, source_target_pairs={{0,4},{4,0},{8,12},{12,8},{16,20},{20,16},{24,28},{28,24},{1,5},{5... | collective-permute-start | bytes 3145736 | tf_op jit(solution)/shard_map/ppermute | solution.py:28
  138.2 25.8 %collective-permute-start.43 = (bf16[512,1024]{1,0:T(8,128)(2,1)}, bf16[512,1024]{1,0:T(8,128)(2,1)S(1)}, u32[]{:S(2)}, u32[]{:S(2)}) collective-permute-start(bf16[512,1024]{1,0:T(8,128)(2,1)} %get-tuple-element.124), channel_id=1, source_target_pairs={{0,8},{4,12},{8,0},{12,4},{16,24},{20,28},{24,16},{28,20},{1,9},{5... | collective-permute-start | bytes 3145736 | tf_op jit(solution)/shard_map/ppermute | solution.py:28
  141.4 22.2 %copy-start.51 = (f32[512,1024]{1,0:T(8,128)S(1)}, f32[512,1024]{1,0:T(8,128)}, u32[]{:S(2)}) copy-start(f32[512,1024]{1,0:T(8,128)} %get-tuple-element.121) | copy-start | bytes 6291460
  161.8 14.8 %collective-permute-start.14 = (bf16[256,1024]{1,0:T(8,128)(2,1)S(1)}, bf16[256,1024]{1,0:T(8,128)(2,1)S(1)}, u32[]{:S(2)}, u32[]{:S(2)}) collective-permute-start(bf16[256,1024]{1,0:T(8,128)(2,1)S(1)} %slice.406), channel_id=1, source_target_pairs={{0,2},{1,3},{2,0},{3,1},{4,6},{5,7},{6,4},{7,5},{8,10},{9,11},{10,... | collective-permute-start | bytes 1572872 | tf_op jit(solution)/shard_map/ppermute | solution.py:28
  164.0 57.5 %collective-permute-start.41 = (bf16[256,1024]{1,0:T(8,128)(2,1)S(1)}, bf16[256,1024]{1,0:T(8,128)(2,1)S(1)}, u32[]{:S(2)}, u32[]{:S(2)}) collective-permute-start(bf16[256,1024]{1,0:T(8,128)(2,1)S(1)} %slice.402), channel_id=1, source_target_pairs={{0,8},{4,12},{8,0},{12,4},{16,24},{20,28},{24,16},{28,20},{1,9},{5... | collective-permute-start | bytes 1572872 | tf_op jit(solution)/shard_map/ppermute | solution.py:28
  166.2 59.1 %collective-permute-start.44 = (bf16[256,1024]{1,0:T(8,128)(2,1)S(1)}, bf16[256,1024]{1,0:T(8,128)(2,1)S(1)}, u32[]{:S(2)}, u32[]{:S(2)}) collective-permute-start(bf16[256,1024]{1,0:T(8,128)(2,1)S(1)} %slice.401), channel_id=1, source_target_pairs={{0,4},{4,0},{8,12},{12,8},{16,20},{20,16},{24,28},{28,24},{1,5},{5... | collective-permute-start | bytes 1572872 | tf_op jit(solution)/shard_map/ppermute | solution.py:28
  170.0 17.9 %collective-permute-start.7 = (bf16[256,1024]{1,0:T(8,128)(2,1)S(1)}, bf16[256,1024]{1,0:T(8,128)(2,1)S(1)}, u32[]{:S(2)}, u32[]{:S(2)}) collective-permute-start(bf16[256,1024]{1,0:T(8,128)(2,1)S(1)} %slice.408), channel_id=1, source_target_pairs={{0,2},{1,3},{2,0},{3,1},{4,6},{5,7},{6,4},{7,5},{8,10},{9,11},{10,... | collective-permute-start | bytes 1572872 | tf_op jit(solution)/shard_map/ppermute | solution.py:28
  173.0 37.9 %collective-permute-start.12 = (bf16[256,1024]{1,0:T(8,128)(2,1)S(1)}, bf16[256,1024]{1,0:T(8,128)(2,1)S(1)}, u32[]{:S(2)}, u32[]{:S(2)}) collective-permute-start(bf16[256,1024]{1,0:T(8,128)(2,1)S(1)} %slice.407), channel_id=1, source_target_pairs={{0,2},{1,3},{2,0},{3,1},{4,6},{5,7},{6,4},{7,5},{8,10},{9,11},{10,... | collective-permute-start | bytes 1572872 | tf_op jit(solution)/shard_map/ppermute | solution.py:28
  176.4 11.4 %copy-start.38 = (bf16[1,1024,1024]{2,1,0:T(8,128)(2,1)S(1)}, bf16[1,1024,1024]{2,1,0:T(8,128)(2,1)}, u32[]{:S(2)}) copy-start(bf16[1,1024,1024]{2,1,0:T(8,128)(2,1)} %get-tuple-element.179) | copy-start | bytes 6291460
  176.6 33.7 %collective-permute-start.21 = (bf16[256,1024]{1,0:T(8,128)(2,1)S(1)}, bf16[256,1024]{1,0:T(8,128)(2,1)S(1)}, u32[]{:S(2)}, u32[]{:S(2)}) collective-permute-start(bf16[256,1024]{1,0:T(8,128)(2,1)S(1)} %slice.404), channel_id=1, source_target_pairs={{0,2},{1,3},{2,0},{3,1},{4,6},{5,7},{6,4},{7,5},{8,10},{9,11},{10,... | collective-permute-start | bytes 1572872 | tf_op jit(solution)/shard_map/ppermute | solution.py:28
  190.3 23.6 %copy-start.16 = (bf16[256,1024]{1,0:T(8,128)(2,1)}, bf16[256,1024]{1,0:T(8,128)(2,1)S(1)}, u32[]{:S(2)}) copy-start(bf16[256,1024]{1,0:T(8,128)(2,1)S(1)} %get-tuple-element.170.u0.refs_2_) | copy-start | bytes 1572868
  190.3 31.2 %collective-permute-start.15 = (bf16[256,1024]{1,0:T(8,128)(2,1)S(1)}, bf16[256,1024]{1,0:T(8,128)(2,1)S(1)}, u32[]{:S(2)}, u32[]{:S(2)}) collective-permute-start(bf16[256,1024]{1,0:T(8,128)(2,1)S(1)} %get-tuple-element.170.u0.refs_2_), channel_id=1, source_target_pairs={{0,2},{1,3},{2,0},{3,1},{4,6},{5,7},{6,4},{7,5},{8,10},{9,11},{10,... | collective-permute-start | bytes 1572872 | tf_op jit(solution)/shard_map/ppermute | solution.py:28
  210.3 15.9 %collective-permute-start.16 = (bf16[256,1024]{1,0:T(8,128)(2,1)S(1)}, bf16[256,1024]{1,0:T(8,128)(2,1)S(1)}, u32[]{:S(2)}, u32[]{:S(2)}) collective-permute-start(bf16[256,1024]{1,0:T(8,128)(2,1)S(1)} %get-tuple-element.170.u0.refs_2_), channel_id=1, source_target_pairs={{0,1},{1,0},{2,3},{3,2},{4,5},{5,4},{6,7},{7,6},{8,9},{9,8},{10,11... | collective-permute-start | bytes 1572872 | tf_op jit(solution)/shard_map/ppermute | solution.py:28
  213.9 12.3 %copy-start.2 = (bf16[256,1024]{1,0:T(8,128)(2,1)}, bf16[256,1024]{1,0:T(8,128)(2,1)S(1)}, u32[]{:S(2)}) copy-start(bf16[256,1024]{1,0:T(8,128)(2,1)S(1)} %get-tuple-element.185.u0.refs_6_) | copy-start | bytes 1572868
  213.9 17.7 %collective-permute-start.22 = (bf16[256,1024]{1,0:T(8,128)(2,1)S(1)}, bf16[256,1024]{1,0:T(8,128)(2,1)S(1)}, u32[]{:S(2)}, u32[]{:S(2)}) collective-permute-start(bf16[256,1024]{1,0:T(8,128)(2,1)S(1)} %get-tuple-element.185.u0.refs_6_), channel_id=1, source_target_pairs={{0,2},{1,3},{2,0},{3,1},{4,6},{5,7},{6,4},{7,5},{8,10},{9,11},{10,... | collective-permute-start | bytes 1572872 | tf_op jit(solution)/shard_map/ppermute | solution.py:28
  221.5 10.1 %collective-permute-start.17 = (bf16[256,1024]{1,0:T(8,128)(2,1)S(1)}, bf16[256,1024]{1,0:T(8,128)(2,1)S(1)}, u32[]{:S(2)}, u32[]{:S(2)}) collective-permute-start(bf16[256,1024]{1,0:T(8,128)(2,1)S(1)} %collective-permute-done.15.u1.refs_3_), channel_id=1, source_target_pairs={{0,1},{1,0},{2,3},{3,2},{4,5},{5,4},{6,7},{7,6},{8,9},{9,8},{10,11... | collective-permute-start | bytes 1572872 | tf_op jit(solution)/shard_map/ppermute | solution.py:28
  222.4 62.6 %collective-permute-start.42 = (bf16[128,1024]{1,0:T(8,128)(2,1)}, bf16[128,1024]{1,0:T(8,128)(2,1)S(1)}, u32[]{:S(2)}, u32[]{:S(2)}) collective-permute-start(bf16[128,1024]{1,0:T(8,128)(2,1)} %slice.411), channel_id=1, source_target_pairs={{0,16},{4,20},{8,24},{12,28},{16,0},{20,4},{24,8},{28,12},{1,17},{... | collective-permute-start | bytes 786440 | tf_op jit(solution)/shard_map/ppermute | solution.py:28
  226.2 56.8 %collective-permute-start.45 = (bf16[128,1024]{1,0:T(8,128)(2,1)}, bf16[128,1024]{1,0:T(8,128)(2,1)}, u32[]{:S(2)}, u32[]{:S(2)}) collective-permute-start(bf16[128,1024]{1,0:T(8,128)(2,1)} %slice.410), channel_id=1, source_target_pairs={{0,16},{4,20},{8,24},{12,28},{16,0},{20,4},{24,8},{28,12},{1,17},{... | collective-permute-start | bytes 786440 | tf_op jit(solution)/shard_map/ppermute | solution.py:28
  226.2 31.3 %collective-permute-start.23 = (bf16[256,1024]{1,0:T(8,128)(2,1)S(1)}, bf16[256,1024]{1,0:T(8,128)(2,1)S(1)}, u32[]{:S(2)}, u32[]{:S(2)}) collective-permute-start(bf16[256,1024]{1,0:T(8,128)(2,1)S(1)} %get-tuple-element.185.u0.refs_6_), channel_id=1, source_target_pairs={{0,1},{1,0},{2,3},{3,2},{4,5},{5,4},{6,7},{7,6},{8,9},{9,8},{10,11... | collective-permute-start | bytes 1572872 | tf_op jit(solution)/shard_map/ppermute | solution.py:28
  231.6 25.4 %copy-start.10 = (bf16[256,1024]{1,0:T(8,128)(2,1)}, bf16[256,1024]{1,0:T(8,128)(2,1)S(1)}, u32[]{:S(2)}) copy-start(bf16[256,1024]{1,0:T(8,128)(2,1)S(1)} %collective-permute-done.22.u1.refs_7_) | copy-start | bytes 1572868
  231.6 25.9 %collective-permute-start.24 = (bf16[256,1024]{1,0:T(8,128)(2,1)S(1)}, bf16[256,1024]{1,0:T(8,128)(2,1)S(1)}, u32[]{:S(2)}, u32[]{:S(2)}) collective-permute-start(bf16[256,1024]{1,0:T(8,128)(2,1)S(1)} %collective-permute-done.22.u1.refs_7_), channel_id=1, source_target_pairs={{0,1},{1,0},{2,3},{3,2},{4,5},{5,4},{6,7},{7,6},{8,9},{9,8},{10,11... | collective-permute-start | bytes 1572872 | tf_op jit(solution)/shard_map/ppermute | solution.py:28
  257.0 54.1 %collective-permute-start.18 = (f32[512,1024]{1,0:T(8,128)}, f32[512,1024]{1,0:T(8,128)}, u32[]{:S(2)}, u32[]{:S(2)}) collective-permute-start(f32[512,1024]{1,0:T(8,128)} %get-tuple-element.87), channel_id=1, source_target_pairs={{0,1},{1,0},{2,3},{3,2},{4,5},{5,4},{6,7},{7,6},{8,9},{9,8},{10,11... | collective-permute-start | bytes 6291464 | tf_op jit(solution)/shard_map/ppermute | solution.py:28
  282.9 32.0 %collective-permute-start.25 = (f32[512,1024]{1,0:T(8,128)}, f32[512,1024]{1,0:T(8,128)}, u32[]{:S(2)}, u32[]{:S(2)}) collective-permute-start(f32[512,1024]{1,0:T(8,128)} %get-tuple-element.92), channel_id=1, source_target_pairs={{0,1},{1,0},{2,3},{3,2},{4,5},{5,4},{6,7},{7,6},{8,9},{9,8},{10,11... | collective-permute-start | bytes 6291464 | tf_op jit(solution)/shard_map/ppermute | solution.py:28
  294.7 16.4 %copy-start.48 = (f32[512,1024]{1,0:T(8,128)S(1)}, f32[512,1024]{1,0:T(8,128)}, u32[]{:S(2)}) copy-start(f32[512,1024]{1,0:T(8,128)} %get-tuple-element.86) | copy-start | bytes 6291460
  309.4 51.7 %collective-permute-start.34 = (bf16[512,768]{1,0:T(8,128)(2,1)}, bf16[512,768]{1,0:T(8,128)(2,1)}, u32[]{:S(2)}, u32[]{:S(2)}) collective-permute-start(bf16[512,768]{1,0:T(8,128)(2,1)} %pad_maximum_fusion.2), channel_id=1, source_target_pairs={{0,8},{4,12},{8,0},{12,4},{16,24},{20,28},{24,16},{28,20},{1,9},{5... | collective-permute-start | bytes 2359304 | tf_op jit(solution)/shard_map/ppermute | solution.py:28
  313.3 14.8 %collective-permute-start.19 = (bf16[256,1024]{1,0:T(8,128)(2,1)S(1)}, bf16[256,1024]{1,0:T(8,128)(2,1)S(1)}, u32[]{:S(2)}, u32[]{:S(2)}) collective-permute-start(bf16[256,1024]{1,0:T(8,128)(2,1)S(1)} %slice.405), channel_id=1, source_target_pairs={{0,2},{1,3},{2,0},{3,1},{4,6},{5,7},{6,4},{7,5},{8,10},{9,11},{10,... | collective-permute-start | bytes 1572872 | tf_op jit(solution)/shard_map/ppermute | solution.py:28
  317.4 21.2 %copy-start.37 = (bf16[1,1024,1024]{2,1,0:T(8,128)(2,1)S(1)}, bf16[1,1024,1024]{2,1,0:T(8,128)(2,1)}, u32[]{:S(2)}) copy-start(bf16[1,1024,1024]{2,1,0:T(8,128)(2,1)} %get-tuple-element.182) | copy-start | bytes 6291460
  317.4 21.2 %collective-permute-start.26 = (bf16[256,1024]{1,0:T(8,128)(2,1)S(1)}, bf16[256,1024]{1,0:T(8,128)(2,1)S(1)}, u32[]{:S(2)}, u32[]{:S(2)}) collective-permute-start(bf16[256,1024]{1,0:T(8,128)(2,1)S(1)} %slice.403), channel_id=1, source_target_pairs={{0,2},{1,3},{2,0},{3,1},{4,6},{5,7},{6,4},{7,5},{8,10},{9,11},{10,... | collective-permute-start | bytes 1572872 | tf_op jit(solution)/shard_map/ppermute | solution.py:28
  320.2 25.5 %collective-permute-start.37 = (bf16[512,256]{1,0:T(8,128)(2,1)S(1)}, bf16[512,256]{1,0:T(8,128)(2,1)}, u32[]{:S(2)}, u32[]{:S(2)}) collective-permute-start(bf16[512,256]{1,0:T(8,128)(2,1)S(1)} %get-tuple-element.112), channel_id=1, source_target_pairs={{0,4},{4,0},{8,12},{12,8},{16,20},{20,16},{24,28},{28,24},{1,5},{5... | collective-permute-start | bytes 786440 | tf_op jit(solution)/shard_map/ppermute | solution.py:28
  345.6 1.5 collective-permute-start.27
  346.7 6.0 %collective-permute-start.38 = (bf16[256,256]{1,0:T(8,128)(2,1)S(1)}, bf16[256,256]{1,0:T(8,128)(2,1)S(1)}, u32[]{:S(2)}, u32[]{:S(2)}) collective-permute-start(bf16[256,256]{1,0:T(8,128)(2,1)S(1)} %slice.413), channel_id=1, source_target_pairs={{0,8},{4,12},{8,0},{12,4},{16,24},{20,28},{24,16},{28,20},{1,9},{5... | collective-permute-start | bytes 393224 | tf_op jit(solution)/shard_map/ppermute | solution.py:28
  347.2 8.2 %collective-permute-start.28 = (f32[2,6144]{1,0:T(2,128)S(1)}, f32[2,6144]{1,0:T(2,128)S(1)}, u32[]{:S(2)}, u32[]{:S(2)}) collective-permute-start(f32[2,6144]{1,0:T(2,128)S(1)} %fusion.62), channel_id=1, source_target_pairs={{0,2},{1,3},{2,0},{3,1},{4,6},{5,7},{6,4},{7,5},{8,10},{9,11},{10,... | collective-permute-start | bytes 147464 | tf_op jit(solution)/shard_map/ppermute | solution.py:28
  352.7 8.4 %copy-start.55 = (f32[512,256]{1,0:T(8,128)S(1)}, f32[512,256]{1,0:T(8,128)}, u32[]{:S(2)}) copy-start(f32[512,256]{1,0:T(8,128)} %get-tuple-element.105) | copy-start | bytes 1572868
  352.7 8.4 %copy-start.56 = (f32[512,256]{1,0:T(8,128)S(1)}, f32[512,256]{1,0:T(8,128)}, u32[]{:S(2)}) copy-start(f32[512,256]{1,0:T(8,128)} %get-tuple-element.106) | copy-start | bytes 1572868
  352.7 8.4 %copy-start.57 = (f32[512,256]{1,0:T(8,128)S(1)}, f32[512,256]{1,0:T(8,128)}, u32[]{:S(2)}) copy-start(f32[512,256]{1,0:T(8,128)} %get-tuple-element.107) | copy-start | bytes 1572868
  352.8 5.9 %collective-permute-start.39 = (bf16[128,256]{1,0:T(8,128)(2,1)S(1)}, bf16[128,256]{1,0:T(8,128)(2,1)S(1)}, u32[]{:S(2)}, u32[]{:S(2)}) collective-permute-start(bf16[128,256]{1,0:T(8,128)(2,1)S(1)} %slice.414), channel_id=1, source_target_pairs={{0,16},{4,20},{8,24},{12,28},{16,0},{20,4},{24,8},{28,12},{1,17},{... | collective-permute-start | bytes 196616 | tf_op jit(solution)/shard_map/ppermute | solution.py:28
  358.2 1.2 collective-permute-start.29
  359.4 4.6 %collective-permute-start.30 = (f32[2,1024]{1,0:T(2,128)S(1)}, f32[2,1024]{1,0:T(2,128)S(1)}, u32[]{:S(2)}, u32[]{:S(2)}) collective-permute-start(f32[2,1024]{1,0:T(2,128)S(1)} %add.463), channel_id=1, source_target_pairs={{0,2},{1,3},{2,0},{3,1},{4,6},{5,7},{6,4},{7,5},{8,10},{9,11},{10,... | collective-permute-start | bytes 24584 | tf_op jit(solution)/shard_map/ppermute | solution.py:28
  362.6 11.2 %collective-permute-start.35 = (bf16[256,768]{1,0:T(8,128)(2,1)S(1)}, bf16[256,768]{1,0:T(8,128)(2,1)S(1)}, u32[]{:S(2)}, u32[]{:S(2)}) collective-permute-start(bf16[256,768]{1,0:T(8,128)(2,1)S(1)} %slice.409), channel_id=1, source_target_pairs={{0,4},{4,0},{8,12},{12,8},{16,20},{20,16},{24,28},{28,24},{1,5},{5... | collective-permute-start | bytes 1179656 | tf_op jit(solution)/shard_map/ppermute | solution.py:28
  364.9 9.5 %collective-permute-start.31 = (f32[8704]{0:T(1024)S(1)}, f32[8704]{0:T(1024)S(1)}, u32[]{:S(2)}, u32[]{:S(2)}) collective-permute-start(f32[8704]{0:T(1024)S(1)} %get-tuple-element.227), channel_id=1, source_target_pairs={{0,4},{4,0},{8,12},{12,8},{16,20},{20,16},{24,28},{28,24},{1,5},{5... | collective-permute-start | bytes 104456 | tf_op jit(solution)/shard_map/ppermute | solution.py:28
  373.8 13.3 %copy-start.42 = (f32[256,1,1024]{2,0,1:T(8,128)S(1)}, f32[256,1,1024]{2,0,1:T(8,128)}, u32[]{:S(2)}) copy-start(f32[256,1,1024]{2,0,1:T(8,128)} %get-tuple-element.198) | copy-start | bytes 3145732
  373.9 13.3 %copy-start.43 = (f32[256,1,1024]{2,0,1:T(8,128)S(1)}, f32[256,1,1024]{2,0,1:T(8,128)}, u32[]{:S(2)}) copy-start(f32[256,1,1024]{2,0,1:T(8,128)} %get-tuple-element.196) | copy-start | bytes 3145732
  373.9 10.4 %collective-permute-start.36 = (bf16[128,768]{1,0:T(8,128)(2,1)S(1)}, bf16[128,768]{1,0:T(8,128)(2,1)S(1)}, u32[]{:S(2)}, u32[]{:S(2)}) collective-permute-start(bf16[128,768]{1,0:T(8,128)(2,1)S(1)} %slice.412), channel_id=1, source_target_pairs={{0,16},{4,20},{8,24},{12,28},{16,0},{20,4},{24,8},{28,12},{1,17},{... | collective-permute-start | bytes 589832 | tf_op jit(solution)/shard_map/ppermute | solution.py:28
  376.5 9.0 %collective-permute-start.32 = (f32[13824]{0:T(1024)}, f32[13824]{0:T(1024)}, u32[]{:S(2)}, u32[]{:S(2)}) collective-permute-start(f32[13824]{0:T(1024)} %pad_maximum_fusion.6), channel_id=1, source_target_pairs={{0,8},{4,12},{8,0},{12,4},{16,24},{20,28},{24,16},{28,20},{1,9},{5... | collective-permute-start | bytes 165896 | tf_op jit(solution)/shard_map/ppermute | solution.py:28
  387.1 5.6 %collective-permute-start.33 = (f32[24064]{0:T(1024)S(1)}, f32[24064]{0:T(1024)S(1)}, u32[]{:S(2)}, u32[]{:S(2)}) collective-permute-start(f32[24064]{0:T(1024)S(1)} %pad_maximum_fusion.4), channel_id=1, source_target_pairs={{0,16},{4,20},{8,24},{12,28},{16,0},{20,4},{24,8},{28,12},{1,17},{... | collective-permute-start | bytes 288776 | tf_op jit(solution)/shard_map/ppermute | solution.py:28
  (64 other events, 259.5 us)
